TPU v7x, 512 devices: a whole 4x8x8 slice. The times are simulated.
512 devices in a mesh: coil: 8 (over y), pencil: 32 (over z, x_lo, core), frame: 2 (over x_hi).
Axes of the slice: x: 4 (x_hi: 2, x_lo: 2; x = x_hi * 2 + x_lo), y: 8, z: 8, core: 2. Of those that a mesh axis runs over, the one named last changes fastest.
Arguments:
- kdata: bfloat16 [2, 8, 2, 96, 256, 256], P('frame', 'coil', None, None, 'pencil'), may hold values from -6 to 6
- sampling: int32 [2, 96, 256], P('frame'), may hold values 0 or 1
- sensitivity: bfloat16 [8, 2, 96, 256, 256], P('coil', None, 'pencil'), may hold values from -3 to 3
- baseline: bfloat16 [2, 96, 256, 256], P(None, 'pencil', ('coil', 'frame')), may hold values from -6 to 6
- ktrans: bfloat16 [96, 256, 256], P('pencil', ('coil', 'frame')), may hold values from 0 to 0.59765625
- plasma_volume: bfloat16 [96, 256, 256], P('pencil', ('coil', 'frame')), may hold values from 0 to 0.29882812
- arterial: float32 [2], P('frame'), may hold values from 0.5 to 4
- arterial_integral: float32 [2], P('frame'), may hold values from 0.5 to 4
Outputs:
- grad_ktrans: float32 [96, 256, 256], P('pencil', ('coil', 'frame'))
- grad_volume: float32 [96, 256, 256], P('pencil', ('coil', 'frame'))
All inputs are finite; a program needn't handle non-finite values. No bound on the sum of `sampling` on one device may be relied on, other than what follows from the above.
Results may differ from a plain program's by a relative error of at most 0.0023.
Values may be sent and summed in bfloat16 or wider, within the bound.
A program may use at most 64 MiB of HBM per device.

v0:
```python
import math

import jax
import jax.numpy as jnp
from jax import lax
from jax.sharding import PartitionSpec as P


def tables(size):
    index = jnp.arange(size, dtype=jnp.int32)
    product = index[:, None] * index[None, :] % size
    angle = product.astype(jnp.float32) * (2.0 * math.pi / size)
    scale = 1.0 / math.sqrt(size)
    return (
        (jnp.cos(angle) * scale).astype(jnp.bfloat16),
        (jnp.sin(angle) * scale).astype(jnp.bfloat16),
    )


def transform_half(pair, form, cos_t, sin_t, sign):
    real_cos = jnp.einsum(form, pair[0], cos_t, preferred_element_type=jnp.float32)
    real_sin = jnp.einsum(form, pair[0], sin_t, preferred_element_type=jnp.float32)
    imag_cos = jnp.einsum(form, pair[1], cos_t, preferred_element_type=jnp.float32)
    imag_sin = jnp.einsum(form, pair[1], sin_t, preferred_element_type=jnp.float32)
    return jnp.stack([real_cos + sign * imag_sin, imag_cos - sign * real_sin])


def transform_full(pair, form, cos_t, sin_t, sign, out_type):
    cosf = cos_t.astype(jnp.float32)
    sinf = sin_t.astype(jnp.float32)
    high = lax.Precision.HIGHEST
    real_cos = jnp.einsum(form, pair[0], cosf, precision=high)
    real_sin = jnp.einsum(form, pair[0], sinf, precision=high)
    imag_cos = jnp.einsum(form, pair[1], cosf, precision=high)
    imag_sin = jnp.einsum(form, pair[1], sinf, precision=high)
    return jnp.stack([real_cos + sign * imag_sin, imag_cos - sign * real_sin]).astype(out_type)


def per_device(
    kdata, sampling, sensitivity, baseline, ktrans, plasma_volume, arterial, arterial_integral
):
    base_full, ktrans_full, volume_full = (
        lax.all_gather(baseline, ("coil", "frame"), axis=2, tiled=True),
        lax.all_gather(ktrans, ("coil", "frame"), axis=1, tiled=True),
        lax.all_gather(plasma_volume, ("coil", "frame"), axis=1, tiled=True),
    )
    cos_x, sin_x = tables(base_full.shape[2])
    cos_y, sin_y = tables(base_full.shape[3])
    cos_z, sin_z = tables(kdata.shape[3])
    weight_k = arterial_integral[0]
    weight_v = arterial[0]
    factor = (
        1.0
        + weight_k * ktrans_full.astype(jnp.float32)
        + weight_v * volume_full.astype(jnp.float32)
    )
    base_re = base_full[0].astype(jnp.float32)
    base_im = base_full[1].astype(jnp.float32)
    frame_re = base_re * factor
    frame_im = base_im * factor
    sens_re = sensitivity[0, 0].astype(jnp.float32)
    sens_im = sensitivity[0, 1].astype(jnp.float32)
    coil = jnp.stack(
        [sens_re * frame_re - sens_im * frame_im, sens_re * frame_im + sens_im * frame_re]
    )
    after_y = transform_full(coil, "zxy,yk->zxk", cos_y, sin_y, 1.0, jnp.float32)
    after_xy = transform_full(after_y, "zxy,xk->zky", cos_x, sin_x, 1.0, jnp.bfloat16)
    lines = lax.all_to_all(after_xy, "pencil", split_axis=2, concat_axis=1, tiled=True)
    kspace = transform_half(lines, "zxy,zk->kxy", cos_z, sin_z, 1.0)
    keep = sampling[0].astype(jnp.float32)[None, :, None, :]
    resid = keep * (kspace - kdata[0, 0].astype(jnp.float32))
    back_z = transform_full(resid, "zxy,zk->kxy", cos_z, sin_z, -1.0, jnp.bfloat16)
    slab = lax.all_to_all(back_z, "pencil", split_axis=1, concat_axis=2, tiled=True)
    back_zx = transform_half(slab, "zxy,xk->zky", cos_x, sin_x, -1.0)
    back = transform_full(back_zx, "zxy,yk->zxk", cos_y, sin_y, -1.0, jnp.float32)
    adj_re = sens_re * back[0] + sens_im * back[1]
    adj_im = sens_re * back[1] - sens_im * back[0]
    projection = base_re * adj_re + base_im * adj_im
    grad_k, grad_v = (
        lax.psum_scatter(weight_k * projection, ("coil", "frame"), scatter_dimension=1, tiled=True),
        lax.psum_scatter(weight_v * projection, ("coil", "frame"), scatter_dimension=1, tiled=True),
    )
    return (grad_k, grad_v)


def solution(mesh):
    in_specs = (
        P("frame", "coil", None, None, "pencil", None),
        P("frame", None, None),
        P("coil", None, "pencil", None, None),
        P(None, "pencil", ("coil", "frame"), None),
        P("pencil", ("coil", "frame"), None),
        P("pencil", ("coil", "frame"), None),
        P("frame"),
        P("frame"),
    )
    out_specs = (P("pencil", ("coil", "frame"), None), P("pencil", ("coil", "frame"), None))
    return jax.shard_map(
        per_device, mesh=mesh, in_specs=in_specs, out_specs=out_specs, check_vma=False
    )
```

profile of v0, /device:TPU:1, one launch (start us, length us, event | category | flops | bytes accessed | tf_op | source)
XLA Modules:
  0.0 643.1 jit_solution(2756641128386546220)
XLA Ops:
  8.5 37.5 %all_gather.10 = bf16[3,256,256]{2,1,0:T(8,128)(2,1)S(1)} all-gather(bf16[3,16,256]{2,1,0:T(8,128)(2,1)} %param.12), channel_id=1, replica_groups=mesh['coil'=8,'pencil'=32,'frame'=2] {'coil','frame'}, dimensions={1}, use_global_device_ids=true | all-gather | bytes 417792 | tf_op jit(solution)/shard_map/all_gather | solution.py:44
  46.1 31.1 %all_gather.11 = bf16[3,256,256]{2,1,0:T(8,128)(2,1)S(1)} all-gather(bf16[3,16,256]{2,1,0:T(8,128)(2,1)} %param.13), channel_id=1, replica_groups=mesh['coil'=8,'pencil'=32,'frame'=2] {'coil','frame'}, dimensions={1}, use_global_device_ids=true | all-gather | bytes 417792 | tf_op jit(solution)/shard_map/all_gather | solution.py:45
  77.2 37.5 %all_gather.9 = bf16[2,3,256,256]{3,2,1,0:T(8,128)(2,1)S(1)} all-gather(bf16[2,3,16,256]{3,2,1,0:T(8,128)(2,1)} %param.11), channel_id=1, replica_groups=mesh['coil'=8,'pencil'=32,'frame'=2] {'coil','frame'}, dimensions={2}, use_global_device_ids=true | all-gather | bytes 835584 | tf_op jit(solution)/shard_map/all_gather | solution.py:43
  114.7 0.5 fusion.16
  115.2 1.4 fusion.59
  116.6 1.4 fusion.57
  118.1 1.5 convolution_add_fusion.3
  119.5 1.5 convolution_subtract_fusion.3
  121.0 1.5 fusion.53
  122.5 1.5 fusion.61
  124.1 1.6 fusion.13
  125.6 1.7 fusion.14
  127.4 0.1 pad_maximum_fusion
  127.5 0.0 copy-start.2
  127.5 1.7 copy.83
  129.2 32.0 %all-to-all-start = ((bf16[2,3,256,256]{3,0,1,2:T(2,128)(2,1)}), bf16[2,3,256,256]{3,0,1,2:T(2,128)(2,1)S(1)}, u32[]{:S(2)}, u32[]{:S(2)}) async-start(bf16[2,3,256,256]{3,0,1,2:T(2,128)(2,1)} %copy.83), calls=%async_computation | async-start | bytes 1572864 | tf_op jit(solution)/shard_map/all_to_all | solution.py:68
  161.2 0.0 reduce-scatter.5.cloned.1.call-start
  161.3 22.5 %all-to-all-done = bf16[2,3,256,256]{3,0,1,2:T(2,128)(2,1)S(1)} async-done(((bf16[2,3,256,256]{3,0,1,2:T(2,128)(2,1)}), bf16[2,3,256,256]{3,0,1,2:T(2,128)(2,1)S(1)}, u32[]{:S(2)}, u32[]{:S(2)}) %all-to-all-start) | async-done | bytes 786464 | tf_op jit(solution)/shard_map/all_to_all | solution.py:68
  183.8 0.1 copy.142
  183.9 0.1 fusion.192
  184.1 0.4 fusion.30
  184.5 0.4 fusion.34
  185.0 0.5 fusion.5
  185.4 0.5 fusion.6
  185.9 0.2 copy-done.1
  186.1 0.3 fusion
  186.4 0.7 convolution_multiply_fusion
  187.1 0.7 convolution_multiply_fusion.1
  187.8 0.7 fusion.11
  188.5 0.7 fusion.12
  189.2 0.1 pad_maximum_fusion.1
  189.3 0.4 copy.92
  189.8 26.2 %all_to_all.30 = bf16[2,96,8,256]{3,2,0,1:T(8,128)(2,1)S(1)} all-to-all(bf16[2,96,8,256]{3,2,0,1:T(8,128)(2,1)S(1)} %copy.92), channel_id=1, replica_groups=mesh['coil'=8,'pencil'=32,'frame'=2] {'pencil'}, dimensions={1} | all-to-all | bytes 1572864 | tf_op jit(solution)/shard_map/all_to_all | solution.py:73
  216.0 0.1 copy.93
  216.0 0.1 fusion.191
  216.1 1.2 fusion.24
  217.3 1.2 fusion.20
  218.6 1.2 fusion.4
  219.8 1.2 fusion.2
  221.1 1.5 convolution_multiply_fusion.3
  222.5 1.5 convolution_multiply_fusion.2
  224.0 1.4 convolution_add_fusion.1
  225.5 3.0 broadcast_multiply_fusion
  228.4 0.0 reduce-scatter.5.cloned.1.call-update
  228.4 0.0 reduce-scatter.3.cloned.1.call-start
  228.5 0.7 reduce-scatter.3.cloned.1.call-update
  229.2 195.3 %reduce-scatter.5.cloned.1.call-done = f32[3,16,256]{2,1,0:T(8,128)} async-done(((f32[3,256,256]{2,1,0:T(8,128)}), f32[3,16,256]{2,1,0:T(8,128)}) %reduce-scatter.5.cloned.1.call-update) | async-done | bytes 49168 | tf_op jit(solution)/shard_map/reduce_scatter | solution.py:81
  424.5 211.8 %reduce-scatter.3.cloned.1.call-done = f32[3,16,256]{2,1,0:T(8,128)} async-done(((f32[3,256,256]{2,1,0:T(8,128)}), f32[3,16,256]{2,1,0:T(8,128)}) %reduce-scatter.3.cloned.1.call-update) | async-done | bytes 49168 | tf_op jit(solution)/shard_map/reduce_scatter | solution.py:80
  (7 shorter events, 0.1 us)
Async XLA Ops:
  7.2 107.5 %copy-start = (bf16[1,2,3,256,256]{4,3,2,1,0:T(8,128)(2,1)S(1)}, bf16[1,2,3,256,256]{4,3,2,1,0:T(8,128)(2,1)}, u32[]{:S(2)}) copy-start(bf16[1,2,3,256,256]{4,3,2,1,0:T(8,128)(2,1)} %param.10) | copy-start | bytes 2359300
  127.5 33.8 %copy-start.2 = (s32[1,96,256]{2,1,0:T(8,128)S(1)}, s32[1,96,256]{2,1,0:T(8,128)}, u32[]{:S(2)}) copy-start(s32[1,96,256]{2,1,0:T(8,128)} %param.9) | copy-start | bytes 294916
  129.2 54.7 %all-to-all-start = ((bf16[2,3,256,256]{3,0,1,2:T(2,128)(2,1)}), bf16[2,3,256,256]{3,0,1,2:T(2,128)(2,1)S(1)}, u32[]{:S(2)}, u32[]{:S(2)}) async-start(bf16[2,3,256,256]{3,0,1,2:T(2,128)(2,1)} %copy.83), calls=%async_computation | async-start | bytes 1572864 | tf_op jit(solution)/shard_map/all_to_all | solution.py:68
  161.2 263.3 %reduce-scatter.5.cloned.1.call-start = ((), (), s32[]{:S(2)}) async-start(), calls=%async_computation.5 | async-start | bytes 835584 | tf_op jit(solution)/shard_map/reduce_scatter | solution.py:81
  185.0 1.1 copy-start.1
  228.4 407.8 %reduce-scatter.3.cloned.1.call-start = ((), (), s32[]{:S(2)}) async-start(), calls=%async_computation.4 | async-start | bytes 835584 | tf_op jit(solution)/shard_map/reduce_scatter | solution.py:80
Sparse Core Ops, SparseCore 0:
  228.6 195.8 reduce-scatter.4
  430.1 206.0 reduce-scatter.2
where the time goes:
time: 647 us; the launch traced here: 643 us
  waiting for transfers between devices  430 us (66%)
  blocking collectives  132 us (20%)
  starting transfers between devices  32.1 us (5%)
  matrix products  29.1 us (4%)
  between operations  15.7 us (2%)
    reduce_scatter x1, waiting for transfers between devices, per_device(): lax.psum_scatter(weight_k * projection, ('coil', 'frame'), scatter_dimens...  212 us
    reduce_scatter x1, waiting for transfers between devices, per_device(): lax.psum_scatter(weight_v * projection, ('coil', 'frame'), scatter_dimens...  195 us
    all_gather x1, blocking collectives, per_device(): lax.all_gather(ktrans, ('coil', 'frame'), axis=1, tiled=True)  37.5 us
    all_gather x1, blocking collectives, per_device(): lax.all_gather(baseline, ('coil', 'frame'), axis=2, tiled=True)  37.5 us
    all_to_all x1, starting transfers between devices, per_device(): lax.all_to_all(after_xy, 'pencil', split_axis=2, concat_axis=1, tiled=True)  32 us
    all_gather x1, blocking collectives, per_device(): lax.all_gather(plasma_volume, ('coil', 'frame'), axis=1, tiled=True)  31.1 us
    all_to_all x1, blocking collectives, per_device(): lax.all_to_all(back_z, 'pencil', split_axis=1, concat_axis=2, tiled=True)  26.2 us
    all_to_all x1, waiting for transfers between devices, per_device(): lax.all_to_all(after_xy, 'pencil', split_axis=2, concat_axis=1, tiled=True)  22.5 us
  transfers between devices with their start and end apart: 3, of which 3 were waited for; matrix products, arithmetic and copies ran while one was open for 0% of the time, Pallas kernels for 0%

commit v1 on v0

v1 whole, which is shorter than its diff:
```python
import math

import jax
import jax.numpy as jnp
import numpy as np
from jax import lax
from jax.experimental import pallas as pl
from jax.experimental.pallas import tpu as pltpu
from jax.sharding import PartitionSpec as P

MESH = pl.DeviceIdType.MESH
F32 = jnp.float32
BF16 = jnp.bfloat16


def tables(size):
    index = np.arange(size)
    product = index[:, None] * index[None, :] % size
    angle = product.astype(np.float32) * np.float32(2.0 * math.pi / size)
    scale = np.float32(1.0 / math.sqrt(size))
    return (
        (np.cos(angle.astype(np.float64)).astype(np.float32) * scale).astype(BF16),
        (np.sin(angle.astype(np.float64)).astype(np.float32) * scale).astype(BF16),
    )


def complex_table(size):
    cos_t, sin_t = tables(size)
    return np.stack(
        [
            np.stack([cos_t.T, sin_t.T], axis=1),
            np.stack([-sin_t.T, cos_t.T], axis=1),
        ]
    )


def all_tables(nx, ny, nz, pencils):
    lines, planes = nx // pencils, nz // pencils
    cos_y, sin_y = tables(ny)
    rows_y = np.concatenate([cos_y, sin_y], axis=1)
    full_x = complex_table(nx)
    forward_x = (
        full_x.reshape(2, pencils, lines, 2 * nx)
        .transpose(1, 0, 2, 3)
        .reshape(2 * nx, 2 * nx)
    )
    inverse_x = np.ascontiguousarray(forward_x.T)
    full_z = complex_table(nz)
    spread = np.einsum(
        "akbz,ij->akibzj", full_z.astype(np.float32), np.eye(lines, dtype=np.float32)
    )
    spread = spread.reshape(2, nz, lines, 2, pencils, planes, lines)
    forward_z = (
        spread.transpose(5, 0, 1, 2, 4, 3, 6)
        .reshape(planes, 2 * nz * lines, pencils * 2 * lines)
        .astype(BF16)
    )
    inverse_z = np.ascontiguousarray(forward_z.transpose(0, 2, 1))
    return rows_y, forward_x, inverse_x, forward_z, inverse_z


def dot(a, b):
    return jnp.dot(a, b, preferred_element_type=F32)


def split(value):
    high = value.astype(BF16)
    return high, (value - high.astype(F32)).astype(BF16)


def kernel(
    sizes,
    base_in,
    ktrans_in,
    volume_in,
    arterial,
    integral,
    sens_in,
    kdata_in,
    sampling_in,
    rows_y_in,
    forward_x_in,
    inverse_x_in,
    forward_z_in,
    inverse_z_in,
    out_k,
    out_v,
    maps,
    sens,
    kdata,
    sampling,
    rows_y,
    forward_x,
    inverse_x,
    forward_z,
    inverse_z,
    field,
    send_f,
    recv_f,
    kspace,
    res_high,
    res_low,
    send_b,
    recv_b,
    send_p,
    recv_p,
    weights,
    own_sem,
    load_sem,
    maps_send,
    maps_recv,
    fsend_sem,
    frecv_sem,
    bsend_sem,
    brecv_sem,
    psend_sem,
    precv_sem,
    wsend_sem,
    wrecv_sem,
):
    coils, pencils, frames = sizes
    planes = maps.shape[0]
    nx = field.shape[2]
    c = lax.axis_index("coil")
    p = lax.axis_index("pencil")
    t = lax.axis_index("frame")
    me = c * frames + t
    other = 1 - t
    right = lax.rem(c + 1, coils)
    left = lax.rem(c + coils - 1, coils)

    own = [
        pltpu.make_async_copy(base_in.at[0], maps.at[:, 0, me], own_sem.at[0]),
        pltpu.make_async_copy(base_in.at[1], maps.at[:, 1, me], own_sem.at[1]),
        pltpu.make_async_copy(ktrans_in, maps.at[:, 2, me], own_sem.at[2]),
        pltpu.make_async_copy(volume_in, maps.at[:, 3, me], own_sem.at[3]),
    ]
    for copy in own:
        copy.start()
    pairs = [
        (rows_y_in, rows_y),
        (sens_in, sens),
        (forward_x_in, forward_x),
        (forward_z_in, forward_z),
        (kdata_in, kdata),
        (sampling_in, sampling),
        (inverse_z_in, inverse_z),
        (inverse_x_in, inverse_x),
    ]
    loads = [
        pltpu.make_async_copy(src, dst, load_sem.at[n])
        for n, (src, dst) in enumerate(pairs)
    ]
    for copy in loads:
        copy.start()

    barrier = pltpu.get_barrier_semaphore()

    def greet_pencil(d, carry):
        peer = lax.rem(p + d, pencils)
        pl.semaphore_signal(barrier, inc=1, device_id={"pencil": peer}, device_id_type=MESH)
        return carry

    lax.fori_loop(1, pencils, greet_pencil, 0)

    def greet_maps(d, carry):
        peer = lax.rem(me + d, coils * frames)
        pl.semaphore_signal(
            barrier,
            inc=1,
            device_id={"coil": peer // frames, "frame": lax.rem(peer, frames)},
            device_id_type=MESH,
        )
        return carry

    lax.fori_loop(1, coils * frames, greet_maps, 0)
    pl.semaphore_wait(barrier, pencils - 1 + coils * frames - 1)

    weights[t, 0] = jnp.full(weights.shape[2:], integral[0], F32)
    weights[t, 1] = jnp.full(weights.shape[2:], arterial[0], F32)
    weight_copy = pltpu.make_async_remote_copy(
        weights.at[t],
        weights.at[t],
        wsend_sem,
        wrecv_sem,
        device_id={"frame": other},
        device_id_type=MESH,
    )
    weight_copy.start()

    def push(i, owner, axis, to):
        pltpu.make_async_remote_copy(
            maps.at[i, :, owner],
            maps.at[i, :, owner],
            maps_send.at[i],
            maps_recv.at[i, owner],
            device_id={axis: to},
            device_id_type=MESH,
        ).start()

    def arrive(i, owner):
        block = maps.at[i, :, owner]
        pltpu.make_async_copy(block, block, maps_recv.at[i, owner]).wait()

    def owner_at(shift, frame):
        return lax.rem(c + shift + coils, coils) * frames + frame

    def gather_start(i):
        push(i, me, "frame", other)
        push(i, me, "coil", right)
        push(i, me, "coil", left)

    def gather_cross(i):
        mine = owner_at(0, other)
        arrive(i, mine)
        push(i, mine, "coil", left)
        push(i, mine, "coil", right)

    half = coils // 2

    def gather_step(i, s):
        for frame, far_right in ((t, True), (other, False)):
            if s < half or far_right:
                owner = owner_at(-s, frame)
                arrive(i, owner)
                if s < (half if far_right else half - 1):
                    push(i, owner, "coil", right)
            if s < half or not far_right:
                owner = owner_at(s, frame)
                arrive(i, owner)
                if s < (half - 1 if far_right else half):
                    push(i, owner, "coil", left)

    def forward(i):
        shape = (nx, maps.shape[-1])
        base_re = maps[i, 0].reshape(shape).astype(F32)
        base_im = maps[i, 1].reshape(shape).astype(F32)
        factor = (
            1.0
            + integral[0] * maps[i, 2].reshape(shape).astype(F32)
            + arterial[0] * maps[i, 3].reshape(shape).astype(F32)
        )
        sens_re = sens[0, i].astype(F32)
        sens_im = sens[1, i].astype(F32)
        field_re = sens_re * base_re - sens_im * base_im
        field_im = sens_re * base_im + sens_im * base_re
        field[i, 0] = field_re
        field[i, 1] = field_im
        high, low = split(jnp.concatenate([field_re * factor, field_im * factor], axis=0))
        y = dot(high, rows_y[...]) + dot(low, rows_y[...])
        ny = shape[1]
        high, low = split(
            jnp.concatenate(
                [y[:nx, :ny] + y[nx:, ny:], y[nx:, :ny] - y[:nx, ny:]], axis=0
            )
        )
        x = dot(forward_x[...], high) + dot(forward_x[...], low)
        send_f[i] = x.astype(BF16).reshape(send_f.shape[1:])
        recv_f[i, p] = send_f[i, p]
        exchange(send_f, recv_f, fsend_sem, frecv_sem, i)

    def exchange(src, dst, send_sem, recv_sem, i):
        def one(d, carry):
            peer = lax.rem(p + d, pencils)
            pltpu.make_async_remote_copy(
                src.at[i, peer],
                dst.at[i, p],
                send_sem.at[i],
                recv_sem.at[i],
                device_id={"pencil": peer},
                device_id_type=MESH,
            ).start()
            return carry

        lax.fori_loop(1, pencils, one, 0)

    def wait_bytes(ref, i, count, sem):
        view = ref.at[i, pl.ds(0, count)]
        pltpu.make_async_copy(view, view, sem.at[i]).wait()

    for copy in own:
        copy.wait()
    for i in range(planes):
        gather_start(i)
    for i in range(planes):
        gather_cross(i)
    for s in range(1, half + 1):
        gather_step(0, s)
    for copy in loads[:3]:
        copy.wait()
    forward(0)
    for i in range(1, planes):
        for s in range(1, half + 1):
            gather_step(i, s)
        forward(i)

    loads[3].wait()
    block = nx
    blocks = kspace.shape[0] // block
    for i in range(planes):
        wait_bytes(recv_f, i, pencils - 1, frecv_sem)
        lines = recv_f[i].reshape(-1, recv_f.shape[-1])

        def add(r, carry):
            rows = pl.ds(pl.multiple_of(r * block, block), block)
            term = dot(forward_z[i, rows, :], lines)
            if i > 0:
                term = term + kspace[rows, :]
            kspace[rows, :] = term
            return carry

        lax.fori_loop(0, blocks, add, 0)
    for copy in loads[4:7]:
        copy.wait()
    some = block // kdata.shape[2]

    def residual(r, carry):
        rows = pl.ds(pl.multiple_of(r * block, block), block)
        part, first = r // (blocks // 2), lax.rem(r, blocks // 2) * some
        first = pl.multiple_of(first, some)
        measured = kdata[part, pl.ds(first, some)].astype(F32)
        keep = sampling[pl.ds(first, some), :].astype(F32)[:, None, :]
        value = keep * (kspace[rows, :].reshape(measured.shape) - measured)
        high, low = split(value.reshape(block, -1))
        res_high[rows, :] = high
        res_low[rows, :] = low
        return carry

    lax.fori_loop(0, blocks, residual, 0)
    for i in range(planes):
        x = dot(inverse_z[i], res_high[...]) + dot(inverse_z[i], res_low[...])
        send_b[i] = x.astype(BF16).reshape(send_b.shape[1:])
        recv_b[i, p] = send_b[i, p]
        exchange(send_b, recv_b, bsend_sem, brecv_sem, i)

    loads[7].wait()
    owners = coils * frames
    for i in range(planes):
        wait_bytes(recv_b, i, pencils - 1, brecv_sem)
        x = dot(inverse_x[...], recv_b[i].reshape(-1, recv_b.shape[-1]))
        high, low = split(x)
        y = dot(high, rows_y[...]) + dot(low, rows_y[...])
        ny = recv_b.shape[-1]
        back_re = y[:nx, :ny] - y[nx:, ny:]
        back_im = y[nx:, :ny] + y[:nx, ny:]
        terms = field[i, 0] * back_re + field[i, 1] * back_im
        send_p[i] = terms.astype(BF16).reshape(send_p.shape[1:])
        recv_p[i, me] = send_p[i, me]

        def hand(d, carry):
            peer = lax.rem(me + d, owners)
            pltpu.make_async_remote_copy(
                send_p.at[i, peer],
                recv_p.at[i, me],
                psend_sem.at[i],
                precv_sem.at[i],
                device_id={"coil": peer // frames, "frame": lax.rem(peer, frames)},
                device_id_type=MESH,
            ).start()
            return carry

        lax.fori_loop(1, owners, hand, 0)

    weight_copy.wait()
    for i in range(planes):
        wait_bytes(recv_p, i, owners - 1, precv_sem)
        totals = [
            sum(recv_p[i, n * frames + f].astype(F32) for n in range(coils))
            for f in range(frames)
        ]
        out_k[i] = sum(weights[f, 0] * totals[f] for f in range(frames))
        out_v[i] = sum(weights[f, 1] * totals[f] for f in range(frames))

    for i in range(planes):
        view = maps.at[i, :, pl.ds(0, owners - 1)]
        pltpu.make_async_copy(view, view, maps_send.at[i]).wait()
        wait_bytes(send_f, i, pencils - 1, fsend_sem)
        wait_bytes(send_b, i, pencils - 1, bsend_sem)
        wait_bytes(send_p, i, owners - 1, psend_sem)


def solution(mesh):
    coils, pencils, frames = mesh.shape["coil"], mesh.shape["pencil"], mesh.shape["frame"]

    def per_device(
        kdata, sampling, sensitivity, baseline, ktrans, plasma_volume, arterial, arterial_integral
    ):
        planes, rows, ny = ktrans.shape
        nx = sensitivity.shape[3]
        nz = kdata.shape[3]
        lines = kdata.shape[4]
        owners = coils * frames
        tabs = all_tables(nx, ny, nz, pencils)
        hbm = pl.BlockSpec(memory_space=pl.ANY)
        smem = pl.BlockSpec(memory_space=pltpu.SMEM)
        vmem = pl.BlockSpec(memory_space=pltpu.VMEM)
        out = jax.ShapeDtypeStruct((planes, rows, ny), F32)
        dma = pltpu.SemaphoreType.DMA
        blocks = (planes, pencils, 2 * lines, ny)
        return pl.pallas_call(
            lambda *refs: kernel((coils, pencils, frames), *refs),
            out_shape=(out, out),
            in_specs=[hbm, hbm, hbm, smem, smem] + [hbm] * 8,
            out_specs=(vmem, vmem),
            scratch_shapes=[
                pltpu.VMEM((planes, 4, owners, rows, ny), BF16),
                pltpu.VMEM((2, planes, nx, ny), BF16),
                pltpu.VMEM((2, nz, lines, ny), BF16),
                pltpu.VMEM((nz, ny), jnp.int32),
                *[pltpu.VMEM(tab.shape, BF16) for tab in tabs],
                pltpu.VMEM((planes, 2, nx, ny), F32),
                pltpu.VMEM(blocks, BF16),
                pltpu.VMEM(blocks, BF16),
                pltpu.VMEM((2 * nz * lines, ny), F32),
                pltpu.VMEM((2 * nz * lines, ny), BF16),
                pltpu.VMEM((2 * nz * lines, ny), BF16),
                pltpu.VMEM(blocks, BF16),
                pltpu.VMEM(blocks, BF16),
                pltpu.VMEM((planes, owners, rows, ny), BF16),
                pltpu.VMEM((planes, owners, rows, ny), BF16),
                pltpu.VMEM((frames, 2, rows, ny), F32),
                dma((4,)),
                dma((8,)),
                dma((planes,)),
                dma((planes, owners)),
                dma((planes,)),
                dma((planes,)),
                dma((planes,)),
                dma((planes,)),
                dma((planes,)),
                dma((planes,)),
                dma,
                dma,
            ],
            compiler_params=pltpu.CompilerParams(
                collective_id=0, has_side_effects=True, vmem_limit_bytes=48 * 1024 * 1024
            ),
        )(
            baseline,
            ktrans,
            plasma_volume,
            arterial,
            arterial_integral,
            sensitivity[0],
            kdata[0, 0],
            sampling[0],
            *[jnp.asarray(tab) for tab in tabs],
        )

    in_specs = (
        P("frame", "coil", None, None, "pencil", None),
        P("frame", None, None),
        P("coil", None, "pencil", None, None),
        P(None, "pencil", ("coil", "frame"), None),
        P("pencil", ("coil", "frame"), None),
        P("pencil", ("coil", "frame"), None),
        P("frame"),
        P("frame"),
    )
    out_specs = (P("pencil", ("coil", "frame"), None), P("pencil", ("coil", "frame"), None))
    return jax.shard_map(
        per_device, mesh=mesh, in_specs=in_specs, out_specs=out_specs, check_vma=False
    )
```

time: 647 us -> 110 us (0.17)
  waiting for transfers between devices: 430 us -> 0 us
  blocking collectives: 132 us -> 0 us
  Pallas kernels: 0 us -> 97.5 us
  starting transfers between devices: 32.1 us -> 0 us
  matrix products: 29.1 us -> 0 us
  between operations: 15.7 us -> 1.95 us
  local copies, waits for them, and re-layouts: 2.66 us -> 9.7 us
    reduce_scatter x2 -> x0, waiting for transfers between devices: 407 us -> none  [the longest x1 212 us: per_device(): lax.psum_scatter(weight_k * projection, ('coil', 'frame'), scatter_dimens...]
    all_gather x3 -> x0, blocking collectives: 106 us -> none  [the longest x1 37.5 us: per_device(): lax.all_gather(ktrans, ('coil', 'frame'), axis=1, tiled=True)]
    pallas_call x0 -> x1, Pallas kernels: none -> 97.5 us  [per_device(): pl.pallas_call(lambda *refs: kernel((coils, pencils, frames), *refs), out...]
    all_to_all x1 -> x0, starting transfers between devices: 32 us -> none  [per_device(): lax.all_to_all(after_xy, 'pencil', split_axis=2, concat_axis=1, tiled=True)]
    dot_general x24 -> x0, matrix products: 29.1 us -> none  [the longest x4 6.64 us: transform_full(): imag_cos = jnp.einsum(form, pair[1], cosf, precision=high)]
    all_to_all x1 -> x0, blocking collectives: 26.2 us -> none  [per_device(): lax.all_to_all(back_z, 'pencil', split_axis=1, concat_axis=2, tiled=True)]
    all_to_all x1 -> x0, waiting for transfers between devices: 22.5 us -> none  [per_device(): lax.all_to_all(after_xy, 'pencil', split_axis=2, concat_axis=1, tiled=True)]
    unnamed x6 -> x20, local copies, waits for them, and re-layouts: 0.22 us -> 9.7 us
  transfers between devices with their start and end apart: 3 -> 0, of which waited for: 3 -> 0; matrix products, arithmetic and copies ran while one was open for 0% -> 0% of each run, Pallas kernels for 0% -> 0%
where the time goes in v1:
time: 110 us; the launch traced here: 109 us
  Pallas kernels  97.5 us (89%)
  local copies, waits for them, and re-layouts  9.7 us (9%)
  between operations  1.95 us (2%)
    pallas_call x1, Pallas kernels, per_device(): pl.pallas_call(lambda *refs: kernel((coils, pencils, frames), *refs), out...  97.5 us
    unnamed x20, local copies, waits for them, and re-layouts  9.7 us

profile of v1, /device:TPU:1, one launch (start us, length us, event | category | flops | bytes accessed | tf_op | source)
XLA Modules:
  0.0 109.1 jit_solution(12209710078548945606)
XLA Ops:
  1.9 0.0 copy-start
  1.9 1.1 %copy-done = bf16[1,2,3,256,256]{4,3,2,1,0:T(8,128)(2,1)S(1)} copy-done((bf16[1,2,3,256,256]{4,3,2,1,0:T(8,128)(2,1)S(1)}, bf16[1,2,3,256,256]{4,3,2,1,0:T(8,128)(2,1)}, u32[]{:S(2)}) %copy-start) | copy-done | bytes 786456
  3.1 0.0 copy-start.1
  3.1 1.1 %copy-done.1 = bf16[1,1,2,96,8,256]{5,4,3,2,1,0:T(8,128)(2,1)S(1)} copy-done((bf16[1,1,2,96,8,256]{5,4,3,2,1,0:T(8,128)(2,1)S(1)}, bf16[1,1,2,96,8,256]{5,4,3,2,1,0:T(8,128)(2,1)}, u32[]{:S(2)}) %copy-start.1) | copy-done | bytes 786456
  4.2 0.0 copy-start.2
  4.2 1.0 copy-done.2
  5.2 0.0 copy-start.3
  5.2 1.0 copy-done.3
  6.3 0.0 copy-start.4
  6.3 0.9 copy-done.4
  7.2 0.0 copy-start.5
  7.2 0.9 copy-done.5
  8.1 0.0 copy-start.6
  8.1 0.8 copy-done.6
  8.9 0.0 copy-start.7
  8.9 0.7 copy-done.7
  9.7 0.0 copy-start.8
  9.7 0.7 copy-done.8
  10.4 97.5 %shard_map.140 = (f32[3,16,256]{2,1,0:T(8,128)S(1)}, f32[3,16,256]{2,1,0:T(8,128)S(1)}) custom-call(bf16[2,3,16,256]{3,2,1,0:T(8,128)(2,1)S(1)} %copy-done.6, bf16[3,16,256]{2,1,0:T(8,128)(2,1)S(1)} %copy-done.7, bf16[3,16,256]{2,1,0:T(8,128)(2,1)S(1)} %copy-done.8, f32[1]{0:T(128)S(6)} %copy.17.refs_3_, f32[1]{0:T(128)S(6)} %copy.18.refs_4_, ...), custom_call_target="tpu_custom_call" | custom-call | tf_op jit(solution)/shard_map/pallas_call | solution.py:400
  107.9 0.6 copy.19
  108.5 0.6 copy.20
Async XLA Ops:
  1.9 1.1 %copy-start = (bf16[1,2,3,256,256]{4,3,2,1,0:T(8,128)(2,1)S(1)}, bf16[1,2,3,256,256]{4,3,2,1,0:T(8,128)(2,1)}, u32[]{:S(2)}) copy-start(bf16[1,2,3,256,256]{4,3,2,1,0:T(8,128)(2,1)} %param.15) | copy-start | bytes 2359300
  3.1 1.1 %copy-start.1 = (bf16[1,1,2,96,8,256]{5,4,3,2,1,0:T(8,128)(2,1)S(1)}, bf16[1,1,2,96,8,256]{5,4,3,2,1,0:T(8,128)(2,1)}, u32[]{:S(2)}) copy-start(bf16[1,1,2,96,8,256]{5,4,3,2,1,0:T(8,128)(2,1)} %param.13) | copy-start | bytes 2359300
  4.2 1.0 copy-start.2
  5.2 1.0 copy-start.3
  6.3 0.9 copy-start.4
  7.2 0.9 copy-start.5
  8.1 0.8 copy-start.6
  8.9 0.7 copy-start.7
  9.7 0.7 copy-start.8

commit v2 on v1

--- a/solution.py
+++ b/solution.py
@@ -85,7 +85,11 @@
     inverse_z_in,
     out_k,
     out_v,
-    maps,
+    own_base,
+    own_params,
+    own_frames,
+    images,
+    bases,
     sens,
     kdata,
     sampling,
@@ -94,7 +98,6 @@
     inverse_x,
     forward_z,
     inverse_z,
-    field,
     send_f,
     recv_f,
     kspace,
@@ -107,8 +110,10 @@
     weights,
     own_sem,
     load_sem,
-    maps_send,
-    maps_recv,
+    isend_sem,
+    irecv_sem,
+    base_send,
+    base_recv,
     fsend_sem,
     frecv_sem,
     bsend_sem,
@@ -119,21 +124,19 @@
     wrecv_sem,
 ):
     coils, pencils, frames = sizes
-    planes = maps.shape[0]
-    nx = field.shape[2]
+    planes, owners = images.shape[:2]
+    nx = sens.shape[2]
     c = lax.axis_index("coil")
     p = lax.axis_index("pencil")
     t = lax.axis_index("frame")
     me = c * frames + t
     other = 1 - t
-    right = lax.rem(c + 1, coils)
-    left = lax.rem(c + coils - 1, coils)
 
     own = [
-        pltpu.make_async_copy(base_in.at[0], maps.at[:, 0, me], own_sem.at[0]),
-        pltpu.make_async_copy(base_in.at[1], maps.at[:, 1, me], own_sem.at[1]),
-        pltpu.make_async_copy(ktrans_in, maps.at[:, 2, me], own_sem.at[2]),
-        pltpu.make_async_copy(volume_in, maps.at[:, 3, me], own_sem.at[3]),
+        pltpu.make_async_copy(base_in.at[0], own_base.at[:, 0], own_sem.at[0]),
+        pltpu.make_async_copy(base_in.at[1], own_base.at[:, 1], own_sem.at[1]),
+        pltpu.make_async_copy(ktrans_in, own_params.at[0], own_sem.at[2]),
+        pltpu.make_async_copy(volume_in, own_params.at[1], own_sem.at[3]),
     ]
     for copy in own:
         copy.start()
@@ -174,10 +177,22 @@
         return carry
 
     lax.fori_loop(1, coils * frames, greet_maps, 0)
-    pl.semaphore_wait(barrier, pencils - 1 + coils * frames - 1)
 
     weights[t, 0] = jnp.full(weights.shape[2:], integral[0], F32)
     weights[t, 1] = jnp.full(weights.shape[2:], arterial[0], F32)
+
+    def frame_rows(frame):
+        factor = (
+            1.0
+            + weights[frame, 0] * own_params[0].astype(F32)
+            + weights[frame, 1] * own_params[1].astype(F32)
+        )
+        own_frames[frame] = (own_base[...].astype(F32) * factor[:, None]).astype(BF16)
+
+    for copy in own:
+        copy.wait()
+    frame_rows(t)
+    pl.semaphore_wait(barrier, pencils - 1 + owners - 1)
     weight_copy = pltpu.make_async_remote_copy(
         weights.at[t],
         weights.at[t],
@@ -188,65 +203,48 @@
     )
     weight_copy.start()
 
-    def push(i, owner, axis, to):
+    def images_to(i, frame, first):
+        def one(d, carry):
+            peer = lax.rem(c + d, coils)
+            pltpu.make_async_remote_copy(
+                own_frames.at[frame, i],
+                images.at[i, me],
+                isend_sem.at[i],
+                irecv_sem.at[i],
+                device_id={"coil": peer, "frame": frame},
+                device_id_type=MESH,
+            ).start()
+            return carry
+
+        lax.fori_loop(first, coils, one, 0)
+
+    def bases_to(d, carry):
+        peer = lax.rem(me + d, owners)
         pltpu.make_async_remote_copy(
-            maps.at[i, :, owner],
-            maps.at[i, :, owner],
-            maps_send.at[i],
-            maps_recv.at[i, owner],
-            device_id={axis: to},
+            own_base,
+            bases.at[me],
+            base_send,
+            base_recv,
+            device_id={"coil": peer // frames, "frame": lax.rem(peer, frames)},
             device_id_type=MESH,
         ).start()
-
-    def arrive(i, owner):
-        block = maps.at[i, :, owner]
-        pltpu.make_async_copy(block, block, maps_recv.at[i, owner]).wait()
-
-    def owner_at(shift, frame):
-        return lax.rem(c + shift + coils, coils) * frames + frame
-
-    def gather_start(i):
-        push(i, me, "frame", other)
-        push(i, me, "coil", right)
-        push(i, me, "coil", left)
-
-    def gather_cross(i):
-        mine = owner_at(0, other)
-        arrive(i, mine)
-        push(i, mine, "coil", left)
-        push(i, mine, "coil", right)
-
-    half = coils // 2
-
-    def gather_step(i, s):
-        for frame, far_right in ((t, True), (other, False)):
-            if s < half or far_right:
-                owner = owner_at(-s, frame)
-                arrive(i, owner)
-                if s < (half if far_right else half - 1):
-                    push(i, owner, "coil", right)
-            if s < half or not far_right:
-                owner = owner_at(s, frame)
-                arrive(i, owner)
-                if s < (half - 1 if far_right else half):
-                    push(i, owner, "coil", left)
+        return carry
 
     def forward(i):
-        shape = (nx, maps.shape[-1])
-        base_re = maps[i, 0].reshape(shape).astype(F32)
-        base_im = maps[i, 1].reshape(shape).astype(F32)
-        factor = (
-            1.0
-            + integral[0] * maps[i, 2].reshape(shape).astype(F32)
-            + arterial[0] * maps[i, 3].reshape(shape).astype(F32)
-        )
+        shape = (nx, images.shape[-1])
+        frame_re = images[i, :, 0].reshape(shape).astype(F32)
+        frame_im = images[i, :, 1].reshape(shape).astype(F32)
         sens_re = sens[0, i].astype(F32)
         sens_im = sens[1, i].astype(F32)
-        field_re = sens_re * base_re - sens_im * base_im
-        field_im = sens_re * base_im + sens_im * base_re
-        field[i, 0] = field_re
-        field[i, 1] = field_im
-        high, low = split(jnp.concatenate([field_re * factor, field_im * factor], axis=0))
+        high, low = split(
+            jnp.concatenate(
+                [
+                    sens_re * frame_re - sens_im * frame_im,
+                    sens_re * frame_im + sens_im * frame_re,
+                ],
+                axis=0,
+            )
+        )
         y = dot(high, rows_y[...]) + dot(low, rows_y[...])
         ny = shape[1]
         high, low = split(
@@ -278,40 +276,35 @@
         view = ref.at[i, pl.ds(0, count)]
         pltpu.make_async_copy(view, view, sem.at[i]).wait()
 
-    for copy in own:
-        copy.wait()
-    for i in range(planes):
-        gather_start(i)
-    for i in range(planes):
-        gather_cross(i)
-    for s in range(1, half + 1):
-        gather_step(0, s)
+    images_to(0, t, 1)
+    weight_copy.wait()
+    frame_rows(other)
+    images_to(0, other, 0)
+    for i in range(1, planes):
+        images_to(i, t, 1)
+        images_to(i, other, 0)
+    images[:, me] = own_frames[t]
+    bases[me] = own_base[...]
     for copy in loads[:3]:
         copy.wait()
-    forward(0)
-    for i in range(1, planes):
-        for s in range(1, half + 1):
-            gather_step(i, s)
+    for i in range(planes):
+        wait_bytes(images, i, owners - 1, irecv_sem)
         forward(i)
+    lax.fori_loop(1, owners, bases_to, 0)
 
     loads[3].wait()
+    for i in range(planes):
+        wait_bytes(recv_f, i, pencils - 1, frecv_sem)
+        lines = recv_f[i].reshape(-1, recv_f.shape[-1])
+
+        term = dot(forward_z[i], lines)
+        if i > 0:
+            term = term + kspace[...]
+        kspace[...] = term
+    for copy in loads[4:7]:
+        copy.wait()
     block = nx
     blocks = kspace.shape[0] // block
-    for i in range(planes):
-        wait_bytes(recv_f, i, pencils - 1, frecv_sem)
-        lines = recv_f[i].reshape(-1, recv_f.shape[-1])
-
-        def add(r, carry):
-            rows = pl.ds(pl.multiple_of(r * block, block), block)
-            term = dot(forward_z[i, rows, :], lines)
-            if i > 0:
-                term = term + kspace[rows, :]
-            kspace[rows, :] = term
-            return carry
-
-        lax.fori_loop(0, blocks, add, 0)
-    for copy in loads[4:7]:
-        copy.wait()
     some = block // kdata.shape[2]
 
     def residual(r, carry):
@@ -334,7 +327,8 @@
         exchange(send_b, recv_b, bsend_sem, brecv_sem, i)
 
     loads[7].wait()
-    owners = coils * frames
+    base_blocks = bases.at[pl.ds(0, owners - 1)]
+    pltpu.make_async_copy(base_blocks, base_blocks, base_recv).wait()
     for i in range(planes):
         wait_bytes(recv_b, i, pencils - 1, brecv_sem)
         x = dot(inverse_x[...], recv_b[i].reshape(-1, recv_b.shape[-1]))
@@ -343,7 +337,13 @@
         ny = recv_b.shape[-1]
         back_re = y[:nx, :ny] - y[nx:, ny:]
         back_im = y[nx:, :ny] + y[:nx, ny:]
-        terms = field[i, 0] * back_re + field[i, 1] * back_im
+        sens_re = sens[0, i].astype(F32)
+        sens_im = sens[1, i].astype(F32)
+        adj_re = sens_re * back_re + sens_im * back_im
+        adj_im = sens_re * back_im - sens_im * back_re
+        base_re = bases[:, i, 0].reshape(nx, ny).astype(F32)
+        base_im = bases[:, i, 1].reshape(nx, ny).astype(F32)
+        terms = base_re * adj_re + base_im * adj_im
         send_p[i] = terms.astype(BF16).reshape(send_p.shape[1:])
         recv_p[i, me] = send_p[i, me]
 
@@ -361,7 +361,6 @@
 
         lax.fori_loop(1, owners, hand, 0)
 
-    weight_copy.wait()
     for i in range(planes):
         wait_bytes(recv_p, i, owners - 1, precv_sem)
         totals = [
@@ -372,11 +371,11 @@
         out_v[i] = sum(weights[f, 1] * totals[f] for f in range(frames))
 
     for i in range(planes):
-        view = maps.at[i, :, pl.ds(0, owners - 1)]
-        pltpu.make_async_copy(view, view, maps_send.at[i]).wait()
+        wait_bytes(images, i, owners - 1, isend_sem)
         wait_bytes(send_f, i, pencils - 1, fsend_sem)
         wait_bytes(send_b, i, pencils - 1, bsend_sem)
         wait_bytes(send_p, i, owners - 1, psend_sem)
+    pltpu.make_async_copy(base_blocks, base_blocks, base_send).wait()
 
 
 def solution(mesh):
@@ -391,7 +390,7 @@
         lines = kdata.shape[4]
         owners = coils * frames
         tabs = all_tables(nx, ny, nz, pencils)
-        hbm = pl.BlockSpec(memory_space=pl.ANY)
+        hbm = pl.BlockSpec(memory_space=pltpu.HBM)
         smem = pl.BlockSpec(memory_space=pltpu.SMEM)
         vmem = pl.BlockSpec(memory_space=pltpu.VMEM)
         out = jax.ShapeDtypeStruct((planes, rows, ny), F32)
@@ -403,12 +402,15 @@
             in_specs=[hbm, hbm, hbm, smem, smem] + [hbm] * 8,
             out_specs=(vmem, vmem),
             scratch_shapes=[
-                pltpu.VMEM((planes, 4, owners, rows, ny), BF16),
+                pltpu.VMEM((planes, 2, rows, ny), BF16),
+                pltpu.VMEM((2, planes, rows, ny), BF16),
+                pltpu.VMEM((frames, planes, 2, rows, ny), BF16),
+                pltpu.VMEM((planes, owners, 2, rows, ny), BF16),
+                pltpu.VMEM((owners, planes, 2, rows, ny), BF16),
                 pltpu.VMEM((2, planes, nx, ny), BF16),
                 pltpu.VMEM((2, nz, lines, ny), BF16),
                 pltpu.VMEM((nz, ny), jnp.int32),
                 *[pltpu.VMEM(tab.shape, BF16) for tab in tabs],
-                pltpu.VMEM((planes, 2, nx, ny), F32),
                 pltpu.VMEM(blocks, BF16),
                 pltpu.VMEM(blocks, BF16),
                 pltpu.VMEM((2 * nz * lines, ny), F32),
@@ -422,7 +424,9 @@
                 dma((4,)),
                 dma((8,)),
                 dma((planes,)),
-                dma((planes, owners)),
+                dma((planes,)),
+                dma,
+                dma,
                 dma((planes,)),
                 dma((planes,)),
                 dma((planes,)),
@@ -433,7 +437,7 @@
                 dma,
             ],
             compiler_params=pltpu.CompilerParams(
-                collective_id=0, has_side_effects=True, vmem_limit_bytes=48 * 1024 * 1024
+                collective_id=0, has_side_effects=True, vmem_limit_bytes=56 * 1024 * 1024
             ),
         )(
             baseline,

time: 110 us -> 84.7 us (0.77)
  Pallas kernels: 97.5 us -> 78.8 us
  local copies, waits for them, and re-layouts: 9.7 us -> 2.84 us
    pallas_call x1, Pallas kernels: 97.5 us -> 78.8 us  [per_device(): pl.pallas_call(lambda *refs: kernel((coils, pencils, frames), *refs), out...]
    unnamed x20 -> x2, local copies, waits for them, and re-layouts: 9.7 us -> 2.84 us
where the time goes in v2:
time: 84.7 us; the launch traced here: 83.6 us
  Pallas kernels  78.8 us (93%)
  local copies, waits for them, and re-layouts  2.84 us (3%)
  between operations  1.93 us (2%)
    pallas_call x1, Pallas kernels, per_device(): pl.pallas_call(lambda *refs: kernel((coils, pencils, frames), *refs), out...  78.8 us
    unnamed x2, local copies, waits for them, and re-layouts  2.84 us

profile of v2, /device:TPU:1, one launch (start us, length us, event | category | flops | bytes accessed | tf_op | source)
XLA Modules:
  0.0 83.6 jit_solution(15426333824814656831)
XLA Ops:
  1.9 78.8 %shard_map.140 = (f32[3,16,256]{2,1,0:T(8,128)}, f32[3,16,256]{2,1,0:T(8,128)}) custom-call(bf16[2,3,16,256]{3,2,1,0:T(8,128)(2,1)} %refs_0_.1, bf16[3,16,256]{2,1,0:T(8,128)(2,1)} %refs_1_.1, bf16[3,16,256]{2,1,0:T(8,128)(2,1)} %refs_2_.1, f32[1]{0:T(128)S(6)} %copy.17.refs_3_, f32[1]{0:T(128)S(6)} %copy.18.refs_4_, bf16[2,3,256,256]{3,2,1,0:T(8,128)(2,1)} %bitcast.3, ...), custom_call_target="tpu_custom_call" | custom-call | tf_op jit(solution)/shard_map/pallas_call | solution.py:399
  80.8 1.4 %copy.19 = f32[3,16,256]{2,1,0:T(8,128)} copy(f32[3,16,256]{2,1,0:T(8,128)} %get-tuple-element.4) | data formatting | bytes 98304
  82.2 1.4 %copy.20 = f32[3,16,256]{2,1,0:T(8,128)} copy(f32[3,16,256]{2,1,0:T(8,128)} %get-tuple-element.5) | data formatting | bytes 98304

commit v3 on v2

--- a/solution.py
+++ b/solution.py
@@ -83,8 +83,7 @@
     inverse_x_in,
     forward_z_in,
     inverse_z_in,
-    out_k,
-    out_v,
+    out,
     own_base,
     own_params,
     own_frames,
@@ -101,8 +100,7 @@
     send_f,
     recv_f,
     kspace,
-    res_high,
-    res_low,
+    residual,
     send_b,
     recv_b,
     send_p,
@@ -125,7 +123,8 @@
 ):
     coils, pencils, frames = sizes
     planes, owners = images.shape[:2]
-    nx = sens.shape[2]
+    nx, ny = sens.shape[2:]
+    halves, width = send_f.shape[1], send_f.shape[-1]
     c = lax.axis_index("coil")
     p = lax.axis_index("pencil")
     t = lax.axis_index("frame")
@@ -140,6 +139,27 @@
     ]
     for copy in own:
         copy.start()
+    barrier = pltpu.get_barrier_semaphore()
+
+    def greet_pencil(d, carry):
+        peer = lax.rem(p + d, pencils)
+        pl.semaphore_signal(barrier, inc=1, device_id={"pencil": peer}, device_id_type=MESH)
+        return carry
+
+    lax.fori_loop(1, pencils, greet_pencil, 0)
+
+    def greet_maps(d, carry):
+        peer = lax.rem(me + d, coils * frames)
+        pl.semaphore_signal(
+            barrier,
+            inc=1,
+            device_id={"coil": peer // frames, "frame": lax.rem(peer, frames)},
+            device_id_type=MESH,
+        )
+        return carry
+
+    lax.fori_loop(1, coils * frames, greet_maps, 0)
+
     pairs = [
         (rows_y_in, rows_y),
         (sens_in, sens),
@@ -157,27 +177,6 @@
     for copy in loads:
         copy.start()
 
-    barrier = pltpu.get_barrier_semaphore()
-
-    def greet_pencil(d, carry):
-        peer = lax.rem(p + d, pencils)
-        pl.semaphore_signal(barrier, inc=1, device_id={"pencil": peer}, device_id_type=MESH)
-        return carry
-
-    lax.fori_loop(1, pencils, greet_pencil, 0)
-
-    def greet_maps(d, carry):
-        peer = lax.rem(me + d, coils * frames)
-        pl.semaphore_signal(
-            barrier,
-            inc=1,
-            device_id={"coil": peer // frames, "frame": lax.rem(peer, frames)},
-            device_id_type=MESH,
-        )
-        return carry
-
-    lax.fori_loop(1, coils * frames, greet_maps, 0)
-
     weights[t, 0] = jnp.full(weights.shape[2:], integral[0], F32)
     weights[t, 1] = jnp.full(weights.shape[2:], arterial[0], F32)
 
@@ -246,31 +245,40 @@
             )
         )
         y = dot(high, rows_y[...]) + dot(low, rows_y[...])
-        ny = shape[1]
         high, low = split(
             jnp.concatenate(
                 [y[:nx, :ny] + y[nx:, ny:], y[nx:, :ny] - y[:nx, ny:]], axis=0
             )
         )
         x = dot(forward_x[...], high) + dot(forward_x[...], low)
-        send_f[i] = x.astype(BF16).reshape(send_f.shape[1:])
-        recv_f[i, p] = send_f[i, p]
-        exchange(send_f, recv_f, fsend_sem, frecv_sem, i)
-
-    def exchange(src, dst, send_sem, recv_sem, i):
+        for h in range(halves):
+            cut = x[:, h * width : (h + 1) * width]
+            send_f[:, h, i] = cut.astype(BF16).reshape(pencils, -1, width)
+        recv_f[p, :, i] = send_f[p, :, i]
+        if i < planes - 1:
+            exchange(send_f, recv_f, fsend_sem, frecv_sem, i, (slice(None), i))
+        else:
+            for h in range(halves):
+                exchange(send_f, recv_f, fsend_sem, frecv_sem, i + h, (h, i))
+
+    def exchange(src, dst, send_sem, recv_sem, n, part):
         def one(d, carry):
             peer = lax.rem(p + d, pencils)
             pltpu.make_async_remote_copy(
-                src.at[i, peer],
-                dst.at[i, p],
-                send_sem.at[i],
-                recv_sem.at[i],
+                src.at[(peer, *part)],
+                dst.at[(p, *part)],
+                send_sem.at[n],
+                recv_sem.at[n],
                 device_id={"pencil": peer},
                 device_id_type=MESH,
             ).start()
             return carry
 
         lax.fori_loop(1, pencils, one, 0)
+
+    def all_but_one(ref, part, sem):
+        view = ref.at[(pl.ds(0, pencils - 1), *part)]
+        pltpu.make_async_copy(view, view, sem).wait()
 
     def wait_bytes(ref, i, count, sem):
         view = ref.at[i, pl.ds(0, count)]
@@ -292,49 +300,52 @@
         forward(i)
     lax.fori_loop(1, owners, bases_to, 0)
 
-    loads[3].wait()
-    for i in range(planes):
-        wait_bytes(recv_f, i, pencils - 1, frecv_sem)
-        lines = recv_f[i].reshape(-1, recv_f.shape[-1])
-
-        term = dot(forward_z[i], lines)
-        if i > 0:
-            term = term + kspace[...]
-        kspace[...] = term
-    for copy in loads[4:7]:
+    for copy in loads[3:6]:
         copy.wait()
-    block = nx
-    blocks = kspace.shape[0] // block
-    some = block // kdata.shape[2]
-
-    def residual(r, carry):
-        rows = pl.ds(pl.multiple_of(r * block, block), block)
-        part, first = r // (blocks // 2), lax.rem(r, blocks // 2) * some
-        first = pl.multiple_of(first, some)
-        measured = kdata[part, pl.ds(first, some)].astype(F32)
-        keep = sampling[pl.ds(first, some), :].astype(F32)[:, None, :]
-        value = keep * (kspace[rows, :].reshape(measured.shape) - measured)
-        high, low = split(value.reshape(block, -1))
-        res_high[rows, :] = high
-        res_low[rows, :] = low
-        return carry
-
-    lax.fori_loop(0, blocks, residual, 0)
-    for i in range(planes):
-        x = dot(inverse_z[i], res_high[...]) + dot(inverse_z[i], res_low[...])
-        send_b[i] = x.astype(BF16).reshape(send_b.shape[1:])
-        recv_b[i, p] = send_b[i, p]
-        exchange(send_b, recv_b, bsend_sem, brecv_sem, i)
+    last = planes - 1
+    for i in range(last):
+        all_but_one(recv_f, (slice(None), i), frecv_sem.at[i])
+        lines = jnp.concatenate(
+            [recv_f[:, h, i].reshape(-1, width) for h in range(halves)], axis=1
+        )
+        if i == 0:
+            so_far = -kdata[...].astype(F32).reshape(kspace.shape)
+        else:
+            so_far = kspace[...]
+        kspace[...] = dot(forward_z[i], lines) + so_far
+    loads[6].wait()
+    half_rows = kspace.shape[0] // 2
+    for h in range(halves):
+        all_but_one(recv_f, (h, last), frecv_sem.at[last + h])
+        lines = recv_f[:, h, last].reshape(-1, width)
+        columns = slice(h * width, (h + 1) * width)
+        keep = sampling[:, columns].astype(F32)[:, None, :]
+        for part in range(2):
+            rows = slice(part * half_rows, (part + 1) * half_rows)
+            value = dot(forward_z[last, rows, :], lines) + kspace[rows, columns]
+            value = keep * value.reshape(keep.shape[0], -1, width)
+            high, low = split(value.reshape(half_rows, width))
+            residual[h, rows, :width] = high
+            residual[h, rows, width:] = low
+        for i in range(planes):
+            x = dot(inverse_z[i], residual[h])
+            x = (x[:, :width] + x[:, width:]).astype(BF16)
+            send_b[:, h, i] = x.reshape(pencils, -1, width)
+            recv_b[p, h, i] = send_b[p, h, i]
+            exchange(send_b, recv_b, bsend_sem, brecv_sem, h * planes + i, (h, i))
 
     loads[7].wait()
     base_blocks = bases.at[pl.ds(0, owners - 1)]
     pltpu.make_async_copy(base_blocks, base_blocks, base_recv).wait()
     for i in range(planes):
-        wait_bytes(recv_b, i, pencils - 1, brecv_sem)
-        x = dot(inverse_x[...], recv_b[i].reshape(-1, recv_b.shape[-1]))
+        for h in range(halves):
+            all_but_one(recv_b, (h, i), brecv_sem.at[h * planes + i])
+        lines = jnp.concatenate(
+            [recv_b[:, h, i].reshape(-1, width) for h in range(halves)], axis=1
+        )
+        x = dot(inverse_x[...], lines)
         high, low = split(x)
         y = dot(high, rows_y[...]) + dot(low, rows_y[...])
-        ny = recv_b.shape[-1]
         back_re = y[:nx, :ny] - y[nx:, ny:]
         back_im = y[nx:, :ny] + y[:nx, ny:]
         sens_re = sens[0, i].astype(F32)
@@ -363,17 +374,20 @@
 
     for i in range(planes):
         wait_bytes(recv_p, i, owners - 1, precv_sem)
-        totals = [
-            sum(recv_p[i, n * frames + f].astype(F32) for n in range(coils))
-            for f in range(frames)
-        ]
-        out_k[i] = sum(weights[f, 0] * totals[f] for f in range(frames))
-        out_v[i] = sum(weights[f, 1] * totals[f] for f in range(frames))
+        for f in range(frames):
+            out[f, i] = sum(recv_p[i, n * frames + f].astype(F32) for n in range(coils))
+    for f in range(frames):
+        out[f, planes, 0:1] = weights[f, 0, 0:1]
+        out[f, planes, 1:2] = weights[f, 1, 0:1]
 
     for i in range(planes):
         wait_bytes(images, i, owners - 1, isend_sem)
-        wait_bytes(send_f, i, pencils - 1, fsend_sem)
-        wait_bytes(send_b, i, pencils - 1, bsend_sem)
+        for h in range(halves):
+            if i == last:
+                all_but_one(send_f, (h, i), fsend_sem.at[last + h])
+            all_but_one(send_b, (h, i), bsend_sem.at[h * planes + i])
+        if i < last:
+            all_but_one(send_f, (slice(None), i), fsend_sem.at[i])
         wait_bytes(send_p, i, owners - 1, psend_sem)
     pltpu.make_async_copy(base_blocks, base_blocks, base_send).wait()
 
@@ -393,14 +407,14 @@
         hbm = pl.BlockSpec(memory_space=pltpu.HBM)
         smem = pl.BlockSpec(memory_space=pltpu.SMEM)
         vmem = pl.BlockSpec(memory_space=pltpu.VMEM)
-        out = jax.ShapeDtypeStruct((planes, rows, ny), F32)
         dma = pltpu.SemaphoreType.DMA
-        blocks = (planes, pencils, 2 * lines, ny)
-        return pl.pallas_call(
+        halves = 2 if ny % 256 == 0 else 1
+        blocks = (pencils, halves, planes, 2 * lines, ny // halves)
+        out = pl.pallas_call(
             lambda *refs: kernel((coils, pencils, frames), *refs),
-            out_shape=(out, out),
+            out_shape=jax.ShapeDtypeStruct((frames, planes + 1, rows, ny), F32),
             in_specs=[hbm, hbm, hbm, smem, smem] + [hbm] * 8,
-            out_specs=(vmem, vmem),
+            out_specs=vmem,
             scratch_shapes=[
                 pltpu.VMEM((planes, 2, rows, ny), BF16),
                 pltpu.VMEM((2, planes, rows, ny), BF16),
@@ -414,8 +428,7 @@
                 pltpu.VMEM(blocks, BF16),
                 pltpu.VMEM(blocks, BF16),
                 pltpu.VMEM((2 * nz * lines, ny), F32),
-                pltpu.VMEM((2 * nz * lines, ny), BF16),
-                pltpu.VMEM((2 * nz * lines, ny), BF16),
+                pltpu.VMEM((halves, 2 * nz * lines, 2 * ny // halves), BF16),
                 pltpu.VMEM(blocks, BF16),
                 pltpu.VMEM(blocks, BF16),
                 pltpu.VMEM((planes, owners, rows, ny), BF16),
@@ -427,10 +440,10 @@
                 dma((planes,)),
                 dma,
                 dma,
-                dma((planes,)),
-                dma((planes,)),
-                dma((planes,)),
-                dma((planes,)),
+                dma((planes - 1 + halves,)),
+                dma((planes - 1 + halves,)),
+                dma((planes * halves,)),
+                dma((planes * halves,)),
                 dma((planes,)),
                 dma((planes,)),
                 dma,
@@ -450,6 +463,10 @@
             sampling[0],
             *[jnp.asarray(tab) for tab in tabs],
         )
+        weights = out[:, planes, :2, 0]
+        return tuple(
+            sum(weights[f, n] * out[f, :planes] for f in range(frames)) for n in range(2)
+        )
 
     in_specs = (
         P("frame", "coil", None, None, "pencil", None),

time: 84.7 us -> 86.8 us (1.025)
  other arithmetic: 0 us -> 3.96 us
  local copies, waits for them, and re-layouts: 2.84 us -> 1.44 us
    add x0 -> x1, other arithmetic: none -> 3.96 us  [per_device(): sum((weights[f, n] * out[f, :planes] for f in range(frames)))]
    unnamed x2 -> x0, local copies, waits for them, and re-layouts: 2.84 us -> none
    slice x0 -> x2, local copies, waits for them, and re-layouts: none -> 1.44 us  [the longest x1 0.79 us: per_device(): weights = out[:, planes, :2, 0]]
where the time goes in v3:
time: 86.8 us; the launch traced here: 86.5 us
  Pallas kernels  79.1 us (91%)
  other arithmetic  3.96 us (5%)
  between operations  1.93 us (2%)
  local copies, waits for them, and re-layouts  1.44 us (2%)
    pallas_call x1, Pallas kernels, per_device(): pl.pallas_call(lambda *refs: kernel((coils, pencils, frames), *refs), out...  79.1 us
    add x1, other arithmetic, per_device(): sum((weights[f, n] * out[f, :planes] for f in range(frames)))  3.96 us

profile of v3, /device:TPU:1, one launch (start us, length us, event | category | flops | bytes accessed | tf_op | source)
XLA Modules:
  0.0 86.5 jit_solution(425349731660187474)
XLA Ops:
  1.9 79.1 %shard_map.140 = f32[2,4,16,256]{3,2,1,0:T(8,128)} custom-call(bf16[2,3,16,256]{3,2,1,0:T(8,128)(2,1)} %refs_0_.1, bf16[3,16,256]{2,1,0:T(8,128)(2,1)} %refs_1_.1, bf16[3,16,256]{2,1,0:T(8,128)(2,1)} %refs_2_.1, f32[1]{0:T(128)S(6)} %copy.15.refs_3_, f32[1]{0:T(128)S(6)} %copy.16.refs_4_, bf16[2,3,256,256]{3,2,1,0:T(8,128)(2,1)} %bitcast.11, ...), custom_call_target="tpu_custom_call" | custom-call | tf_op jit(solution)/shard_map/pallas_call | solution.py:413
  81.1 0.8 slice_reduce_fusion
  81.9 0.7 fusion
  82.5 4.0 %add_bitcast_fusion = (f32[3,16,256]{2,1,0:T(8,128)}, f32[3,16,256]{2,1,0:T(8,128)}) fusion(f32[2,4,16,256]{3,2,1,0:T(8,128)} %shard_map.140, f32[]{:T(128)} %bitcast.7, f32[]{:T(128)} %bitcast.6, f32[]{:T(128)} %bitcast.4, f32[]{:T(128)} %bitcast.3), kind=kLoop, calls=%fused_computation | loop fusion | flops 73728 | bytes 196624 | tf_op jit(solution)/shard_map/add | solution.py:468

commit v4 on v3

--- a/solution.py
+++ b/solution.py
@@ -110,6 +110,7 @@
     load_sem,
     isend_sem,
     irecv_sem,
+    relay_sem,
     base_send,
     base_recv,
     fsend_sem,
@@ -202,20 +203,36 @@
     )
     weight_copy.start()
 
-    def images_to(i, frame, first):
-        def one(d, carry):
-            peer = lax.rem(c + d, coils)
-            pltpu.make_async_remote_copy(
-                own_frames.at[frame, i],
-                images.at[i, me],
-                isend_sem.at[i],
-                irecv_sem.at[i],
-                device_id={"coil": peer, "frame": frame},
-                device_id_type=MESH,
-            ).start()
-            return carry
-
-        lax.fori_loop(first, coils, one, 0)
+    def image_copy(block, i, sem, coil, frame):
+        pltpu.make_async_remote_copy(
+            block,
+            images.at[i, me] if frame is not None else block,
+            isend_sem.at[i],
+            sem,
+            device_id={"coil": lax.rem(coil + coils, coils)}
+            | ({} if frame is None else {"frame": frame}),
+            device_id_type=MESH,
+        ).start()
+
+    def images_to(i, frame):
+        block = own_frames.at[frame, i]
+        image_copy(block, i, relay_sem.at[i, t, 0], c + 2, frame)
+        image_copy(block, i, relay_sem.at[i, t, 1], c - 2, frame)
+        image_copy(block, i, irecv_sem.at[i], c + 1, frame)
+        image_copy(block, i, irecv_sem.at[i], c - 1, frame)
+        if frame is other:
+            image_copy(block, i, irecv_sem.at[i], c, frame)
+
+    def relay(i):
+        for way, step in ((0, 1), (1, -1)):
+            for frame in (t, other):
+                block = images.at[
+                    i, lax.rem(c - 2 * step + coils, coils) * frames + frame
+                ]
+                pltpu.make_async_copy(block, block, relay_sem.at[i, frame, way]).wait()
+                image_copy(block, i, irecv_sem.at[i], c + step, None)
+                if (way == 0) == (frame is t):
+                    image_copy(block, i, irecv_sem.at[i], c + 2 * step, None)
 
     def bases_to(d, carry):
         peer = lax.rem(me + d, owners)
@@ -228,6 +245,12 @@
             device_id_type=MESH,
         ).start()
         return carry
+
+    slabs = [(h, i) for h in range(halves) for i in range(1, planes)]
+    parts = [(slice(None), 0), *slabs]
+
+    def send_forward(n):
+        exchange(send_f, recv_f, fsend_sem, frecv_sem, n, parts[n])
 
     def forward(i):
         shape = (nx, images.shape[-1])
@@ -255,11 +278,13 @@
             cut = x[:, h * width : (h + 1) * width]
             send_f[:, h, i] = cut.astype(BF16).reshape(pencils, -1, width)
         recv_f[p, :, i] = send_f[p, :, i]
-        if i < planes - 1:
-            exchange(send_f, recv_f, fsend_sem, frecv_sem, i, (slice(None), i))
+        if i == 0:
+            send_forward(0)
         else:
-            for h in range(halves):
-                exchange(send_f, recv_f, fsend_sem, frecv_sem, i + h, (h, i))
+            send_forward(1 + slabs.index((0, i)))
+        if i == planes - 1:
+            for n in range(planes, len(slabs) + 1):
+                send_forward(n)
 
     def exchange(src, dst, send_sem, recv_sem, n, part):
         def one(d, carry):
@@ -284,45 +309,47 @@
         view = ref.at[i, pl.ds(0, count)]
         pltpu.make_async_copy(view, view, sem.at[i]).wait()
 
-    images_to(0, t, 1)
+    images_to(0, t)
+    images_to(1, t)
     weight_copy.wait()
     frame_rows(other)
-    images_to(0, other, 0)
-    for i in range(1, planes):
-        images_to(i, t, 1)
-        images_to(i, other, 0)
+    images_to(0, other)
+    images_to(1, other)
+    for i in range(2, planes):
+        images_to(i, t)
+        images_to(i, other)
     images[:, me] = own_frames[t]
     bases[me] = own_base[...]
     for copy in loads[:3]:
         copy.wait()
+    relay(0)
     for i in range(planes):
-        wait_bytes(images, i, owners - 1, irecv_sem)
+        if i < planes - 1:
+            relay(i + 1)
+        wait_bytes(images, i, owners - 5, irecv_sem)
         forward(i)
     lax.fori_loop(1, owners, bases_to, 0)
 
     for copy in loads[3:6]:
         copy.wait()
-    last = planes - 1
-    for i in range(last):
-        all_but_one(recv_f, (slice(None), i), frecv_sem.at[i])
-        lines = jnp.concatenate(
-            [recv_f[:, h, i].reshape(-1, width) for h in range(halves)], axis=1
-        )
-        if i == 0:
-            so_far = -kdata[...].astype(F32).reshape(kspace.shape)
-        else:
-            so_far = kspace[...]
-        kspace[...] = dot(forward_z[i], lines) + so_far
+    all_but_one(recv_f, parts[0], frecv_sem.at[0])
+    lines = jnp.concatenate(
+        [recv_f[:, h, 0].reshape(-1, width) for h in range(halves)], axis=1
+    )
+    kspace[...] = dot(forward_z[0], lines) - kdata[...].astype(F32).reshape(kspace.shape)
     loads[6].wait()
     half_rows = kspace.shape[0] // 2
     for h in range(halves):
-        all_but_one(recv_f, (h, last), frecv_sem.at[last + h])
-        lines = recv_f[:, h, last].reshape(-1, width)
         columns = slice(h * width, (h + 1) * width)
+        for i in range(1, planes):
+            all_but_one(recv_f, (h, i), frecv_sem.at[1 + slabs.index((h, i))])
+            lines = recv_f[:, h, i].reshape(-1, width)
+            if i < planes - 1:
+                kspace[:, columns] = dot(forward_z[i], lines) + kspace[:, columns]
         keep = sampling[:, columns].astype(F32)[:, None, :]
         for part in range(2):
             rows = slice(part * half_rows, (part + 1) * half_rows)
-            value = dot(forward_z[last, rows, :], lines) + kspace[rows, columns]
+            value = dot(forward_z[planes - 1, rows, :], lines) + kspace[rows, columns]
             value = keep * value.reshape(keep.shape[0], -1, width)
             high, low = split(value.reshape(half_rows, width))
             residual[h, rows, :width] = high
@@ -375,20 +402,17 @@
     for i in range(planes):
         wait_bytes(recv_p, i, owners - 1, precv_sem)
         for f in range(frames):
-            out[f, i] = sum(recv_p[i, n * frames + f].astype(F32) for n in range(coils))
-    for f in range(frames):
-        out[f, planes, 0:1] = weights[f, 0, 0:1]
-        out[f, planes, 1:2] = weights[f, 1, 0:1]
+            total = sum(recv_p[i, n * frames + f].astype(F32) for n in range(coils))
+            for n in range(2):
+                out[n, f, i] = weights[f, n] * total
 
     for i in range(planes):
         wait_bytes(images, i, owners - 1, isend_sem)
         for h in range(halves):
-            if i == last:
-                all_but_one(send_f, (h, i), fsend_sem.at[last + h])
             all_but_one(send_b, (h, i), bsend_sem.at[h * planes + i])
-        if i < last:
-            all_but_one(send_f, (slice(None), i), fsend_sem.at[i])
         wait_bytes(send_p, i, owners - 1, psend_sem)
+    for n, part in enumerate(parts):
+        all_but_one(send_f, part, fsend_sem.at[n])
     pltpu.make_async_copy(base_blocks, base_blocks, base_send).wait()
 
 
@@ -412,7 +436,7 @@
         blocks = (pencils, halves, planes, 2 * lines, ny // halves)
         out = pl.pallas_call(
             lambda *refs: kernel((coils, pencils, frames), *refs),
-            out_shape=jax.ShapeDtypeStruct((frames, planes + 1, rows, ny), F32),
+            out_shape=jax.ShapeDtypeStruct((2, frames, planes, rows, ny), F32),
             in_specs=[hbm, hbm, hbm, smem, smem] + [hbm] * 8,
             out_specs=vmem,
             scratch_shapes=[
@@ -438,10 +462,11 @@
                 dma((8,)),
                 dma((planes,)),
                 dma((planes,)),
+                dma((planes, frames, 2)),
                 dma,
                 dma,
-                dma((planes - 1 + halves,)),
-                dma((planes - 1 + halves,)),
+                dma((1 + halves * (planes - 1),)),
+                dma((1 + halves * (planes - 1),)),
                 dma((planes * halves,)),
                 dma((planes * halves,)),
                 dma((planes,)),
@@ -463,10 +488,7 @@
             sampling[0],
             *[jnp.asarray(tab) for tab in tabs],
         )
-        weights = out[:, planes, :2, 0]
-        return tuple(
-            sum(weights[f, n] * out[f, :planes] for f in range(frames)) for n in range(2)
-        )
+        return tuple(sum(out[n, f] for f in range(frames)) for n in range(2))
 
     in_specs = (
         P("frame", "coil", None, None, "pencil", None),

time: 86.8 us -> 81.2 us (0.935)
  other arithmetic: 3.96 us -> 1.52 us
  Pallas kernels: 79.1 us -> 77.5 us
  local copies, waits for them, and re-layouts: 1.44 us -> 0 us
    add x1, other arithmetic: 3.96 us -> 1.52 us  [per_device(): return tuple((sum((out[n, f] for f in range(frames))) for n in range(2)))]
    pallas_call x1, Pallas kernels: 79.1 us -> 77.5 us  [per_device(): pl.pallas_call(lambda *refs: kernel((coils, pencils, frames), *refs), out...]
    slice x2 -> x0, local copies, waits for them, and re-layouts: 1.44 us -> none  [the longest x1 0.79 us: per_device(): weights = out[:, planes, :2, 0]]
where the time goes in v4:
time: 81.2 us; the launch traced here: 81 us
  Pallas kernels  77.5 us (95%)
  between operations  1.93 us (2%)
  other arithmetic  1.52 us (2%)
    pallas_call x1, Pallas kernels, per_device(): pl.pallas_call(lambda *refs: kernel((coils, pencils, frames), *refs), out...  77.5 us

profile of v4, /device:TPU:1, one launch (start us, length us, event | category | flops | bytes accessed | tf_op | source)
XLA Modules:
  0.0 81.0 jit_solution(17869270642631545396)
XLA Ops:
  1.9 77.5 %shard_map.140 = f32[2,2,3,16,256]{4,3,2,1,0:T(8,128)} custom-call(bf16[2,3,16,256]{3,2,1,0:T(8,128)(2,1)} %refs_0_.1, bf16[3,16,256]{2,1,0:T(8,128)(2,1)} %refs_1_.1, bf16[3,16,256]{2,1,0:T(8,128)(2,1)} %refs_2_.1, f32[1]{0:T(128)S(6)} %copy.15.refs_3_, f32[1]{0:T(128)S(6)} %copy.16.refs_4_, bf16[2,3,256,256]{3,2,1,0:T(8,128)(2,1)} %bitcast.7, ...), custom_call_target="tpu_custom_call" | custom-call | tf_op jit(solution)/shard_map/pallas_call | solution.py:437
  79.5 1.5 %add_bitcast_fusion = (f32[3,16,256]{2,1,0:T(8,128)}, f32[3,16,256]{2,1,0:T(8,128)}) fusion(f32[2,2,3,16,256]{4,3,2,1,0:T(8,128)} %shard_map.140), kind=kLoop, calls=%fused_computation | loop fusion | flops 24576 | bytes 294912 | tf_op jit(solution)/shard_map/add | solution.py:491

commit v5 on v4

--- a/solution.py
+++ b/solution.py
@@ -252,6 +252,9 @@
     def send_forward(n):
         exchange(send_f, recv_f, fsend_sem, frecv_sem, n, parts[n])
 
+    def send_left(n):
+        all_but_one(send_f, parts[n], fsend_sem.at[n])
+
     def forward(i):
         shape = (nx, images.shape[-1])
         frame_re = images[i, :, 0].reshape(shape).astype(F32)
@@ -278,13 +281,7 @@
             cut = x[:, h * width : (h + 1) * width]
             send_f[:, h, i] = cut.astype(BF16).reshape(pencils, -1, width)
         recv_f[p, :, i] = send_f[p, :, i]
-        if i == 0:
-            send_forward(0)
-        else:
-            send_forward(1 + slabs.index((0, i)))
-        if i == planes - 1:
-            for n in range(planes, len(slabs) + 1):
-                send_forward(n)
+        send_forward(i)
 
     def exchange(src, dst, send_sem, recv_sem, n, part):
         def one(d, carry):
@@ -310,35 +307,40 @@
         pltpu.make_async_copy(view, view, sem.at[i]).wait()
 
     images_to(0, t)
-    images_to(1, t)
     weight_copy.wait()
     frame_rows(other)
     images_to(0, other)
-    images_to(1, other)
-    for i in range(2, planes):
-        images_to(i, t)
-        images_to(i, other)
     images[:, me] = own_frames[t]
     bases[me] = own_base[...]
     for copy in loads[:3]:
         copy.wait()
-    relay(0)
     for i in range(planes):
+        relay(i)
         if i < planes - 1:
-            relay(i + 1)
+            images_to(i + 1, t)
+            images_to(i + 1, other)
         wait_bytes(images, i, owners - 5, irecv_sem)
         forward(i)
     lax.fori_loop(1, owners, bases_to, 0)
 
     for copy in loads[3:6]:
         copy.wait()
-    all_but_one(recv_f, parts[0], frecv_sem.at[0])
-    lines = jnp.concatenate(
-        [recv_f[:, h, 0].reshape(-1, width) for h in range(halves)], axis=1
-    )
-    kspace[...] = dot(forward_z[0], lines) - kdata[...].astype(F32).reshape(kspace.shape)
+    for n in range(planes, len(parts)):
+        if n == len(parts) - 1:
+            all_but_one(recv_f, parts[0], frecv_sem.at[0])
+            lines = jnp.concatenate(
+                [recv_f[:, h, 0].reshape(-1, width) for h in range(halves)], axis=1
+            )
+            measured = kdata[...].astype(F32).reshape(kspace.shape)
+            kspace[...] = dot(forward_z[0], lines) - measured
+        send_left(n - 2)
+        send_forward(n)
     loads[6].wait()
     half_rows = kspace.shape[0] // 2
+
+    def sent_back(n):
+        all_but_one(send_b, (n // planes, n % planes), bsend_sem.at[n])
+
     for h in range(halves):
         columns = slice(h * width, (h + 1) * width)
         for i in range(1, planes):
@@ -359,7 +361,10 @@
             x = (x[:, :width] + x[:, width:]).astype(BF16)
             send_b[:, h, i] = x.reshape(pencils, -1, width)
             recv_b[p, h, i] = send_b[p, h, i]
-            exchange(send_b, recv_b, bsend_sem, brecv_sem, h * planes + i, (h, i))
+            n = h * planes + i
+            if n >= 2:
+                sent_back(n - 2)
+            exchange(send_b, recv_b, bsend_sem, brecv_sem, n, (h, i))
 
     loads[7].wait()
     base_blocks = bases.at[pl.ds(0, owners - 1)]
@@ -408,11 +413,11 @@
 
     for i in range(planes):
         wait_bytes(images, i, owners - 1, isend_sem)
-        for h in range(halves):
-            all_but_one(send_b, (h, i), bsend_sem.at[h * planes + i])
         wait_bytes(send_p, i, owners - 1, psend_sem)
-    for n, part in enumerate(parts):
-        all_but_one(send_f, part, fsend_sem.at[n])
+    for n in (*range(planes - 2), len(parts) - 2, len(parts) - 1):
+        send_left(n)
+    for n in range(halves * planes - 2, halves * planes):
+        sent_back(n)
     pltpu.make_async_copy(base_blocks, base_blocks, base_send).wait()
 
 

time: 81.2 us -> 85.4 us (1.052)
  Pallas kernels: 77.5 us -> 81.7 us
    pallas_call x1, Pallas kernels: 77.5 us -> 81.7 us  [per_device(): pl.pallas_call(lambda *refs: kernel((coils, pencils, frames), *refs), out...]
where the time goes in v5:
time: 85.4 us; the launch traced here: 85.2 us
  Pallas kernels  81.7 us (96%)
  between operations  1.93 us (2%)
  other arithmetic  1.52 us (2%)
    pallas_call x1, Pallas kernels, per_device(): pl.pallas_call(lambda *refs: kernel((coils, pencils, frames), *refs), out...  81.7 us

profile of v5, /device:TPU:1, one launch (start us, length us, event | category | flops | bytes accessed | tf_op | source)
XLA Modules:
  0.0 85.2 jit_solution(4836024994492934604)
XLA Ops:
  1.9 81.7 %shard_map.140 = f32[2,2,3,16,256]{4,3,2,1,0:T(8,128)} custom-call(bf16[2,3,16,256]{3,2,1,0:T(8,128)(2,1)} %refs_0_.1, bf16[3,16,256]{2,1,0:T(8,128)(2,1)} %refs_1_.1, bf16[3,16,256]{2,1,0:T(8,128)(2,1)} %refs_2_.1, f32[1]{0:T(128)S(6)} %copy.15.refs_3_, f32[1]{0:T(128)S(6)} %copy.16.refs_4_, bf16[2,3,256,256]{3,2,1,0:T(8,128)(2,1)} %bitcast.7, ...), custom_call_target="tpu_custom_call" | custom-call | tf_op jit(solution)/shard_map/pallas_call | solution.py:442
  83.6 1.5 %add_bitcast_fusion = (f32[3,16,256]{2,1,0:T(8,128)}, f32[3,16,256]{2,1,0:T(8,128)}) fusion(f32[2,2,3,16,256]{4,3,2,1,0:T(8,128)} %shard_map.140), kind=kLoop, calls=%fused_computation | loop fusion | flops 24576 | bytes 294912 | tf_op jit(solution)/shard_map/add | solution.py:496

commit v6 on v4

--- a/solution.py
+++ b/solution.py
@@ -66,6 +66,10 @@
 def split(value):
     high = value.astype(BF16)
     return high, (value - high.astype(F32)).astype(BF16)
+
+
+def far_first(n, size):
+    return size // 2 + (1 - 2 * lax.rem(n, 2)) * ((n + 1) // 2)
 
 
 def kernel(
@@ -203,6 +207,30 @@
     )
     weight_copy.start()
 
+    near = 4
+
+    def far_pencil(n):
+        ring = lax.rem(p // near + far_first(n // near, pencils // near), pencils // near)
+        return ring * near + lax.rem(lax.rem(p, near) + lax.rem(n + 1, near), near)
+
+    def far_owner(n):
+        coil = lax.rem(c + far_first(n // frames, coils), coils)
+        return coil, lax.rem(t + lax.rem(n + 1, frames), frames)
+
+    def images_direct(frame, count):
+        def one(n, carry):
+            pltpu.make_async_remote_copy(
+                own_frames.at[frame, 0],
+                images.at[0, me],
+                isend_sem.at[0],
+                irecv_sem.at[0],
+                device_id={"coil": lax.rem(c + far_first(n, coils), coils), "frame": frame},
+                device_id_type=MESH,
+            ).start()
+            return carry
+
+        lax.fori_loop(0, count, one, 0)
+
     def image_copy(block, i, sem, coil, frame):
         pltpu.make_async_remote_copy(
             block,
@@ -287,8 +315,8 @@
                 send_forward(n)
 
     def exchange(src, dst, send_sem, recv_sem, n, part):
-        def one(d, carry):
-            peer = lax.rem(p + d, pencils)
+        def one(n_peer, carry):
+            peer = far_pencil(n_peer)
             pltpu.make_async_remote_copy(
                 src.at[(peer, *part)],
                 dst.at[(p, *part)],
@@ -299,7 +327,7 @@
             ).start()
             return carry
 
-        lax.fori_loop(1, pencils, one, 0)
+        lax.fori_loop(0, pencils - 1, one, 0)
 
     def all_but_one(ref, part, sem):
         view = ref.at[(pl.ds(0, pencils - 1), *part)]
@@ -309,25 +337,23 @@
         view = ref.at[i, pl.ds(0, count)]
         pltpu.make_async_copy(view, view, sem.at[i]).wait()
 
-    images_to(0, t)
-    images_to(1, t)
+    images_direct(t, coils - 1)
     weight_copy.wait()
     frame_rows(other)
-    images_to(0, other)
-    images_to(1, other)
-    for i in range(2, planes):
+    images_direct(other, coils)
+    for i in range(1, planes):
         images_to(i, t)
         images_to(i, other)
     images[:, me] = own_frames[t]
     bases[me] = own_base[...]
     for copy in loads[:3]:
         copy.wait()
-    relay(0)
     for i in range(planes):
-        if i < planes - 1:
-            relay(i + 1)
-        wait_bytes(images, i, owners - 5, irecv_sem)
+        wait_bytes(images, i, owners - (1 if i == 0 else 5), irecv_sem)
         forward(i)
+        if i == 0:
+            for later in range(1, planes):
+                relay(later)
     lax.fori_loop(1, owners, bases_to, 0)
 
     for copy in loads[3:6]:
@@ -385,19 +411,19 @@
         send_p[i] = terms.astype(BF16).reshape(send_p.shape[1:])
         recv_p[i, me] = send_p[i, me]
 
-        def hand(d, carry):
-            peer = lax.rem(me + d, owners)
+        def hand(n, carry):
+            coil, frame = far_owner(n)
             pltpu.make_async_remote_copy(
-                send_p.at[i, peer],
+                send_p.at[i, coil * frames + frame],
                 recv_p.at[i, me],
                 psend_sem.at[i],
                 precv_sem.at[i],
-                device_id={"coil": peer // frames, "frame": lax.rem(peer, frames)},
+                device_id={"coil": coil, "frame": frame},
                 device_id_type=MESH,
             ).start()
             return carry
 
-        lax.fori_loop(1, owners, hand, 0)
+        lax.fori_loop(0, owners - 1, hand, 0)
 
     for i in range(planes):
         wait_bytes(recv_p, i, owners - 1, precv_sem)

time: 81.2 us -> 80.5 us (level)
  no operation moved by 1% of the time
where the time goes in v6:
time: 80.5 us; the launch traced here: 80.3 us
  Pallas kernels  76.9 us (96%)
  between operations  1.93 us (2%)
  other arithmetic  1.52 us (2%)
    pallas_call x1, Pallas kernels, per_device(): pl.pallas_call(lambda *refs: kernel((coils, pencils, frames), *refs), out...  76.9 us

profile of v6, /device:TPU:1, one launch (start us, length us, event | category | flops | bytes accessed | tf_op | source)
XLA Modules:
  0.0 80.3 jit_solution(5082578792682442260)
XLA Ops:
  1.9 76.9 %shard_map.140 = f32[2,2,3,16,256]{4,3,2,1,0:T(8,128)} custom-call(bf16[2,3,16,256]{3,2,1,0:T(8,128)(2,1)} %refs_0_.1, bf16[3,16,256]{2,1,0:T(8,128)(2,1)} %refs_1_.1, bf16[3,16,256]{2,1,0:T(8,128)(2,1)} %refs_2_.1, f32[1]{0:T(128)S(6)} %copy.15.refs_3_, f32[1]{0:T(128)S(6)} %copy.16.refs_4_, bf16[2,3,256,256]{3,2,1,0:T(8,128)(2,1)} %bitcast.7, ...), custom_call_target="tpu_custom_call" | custom-call | tf_op jit(solution)/shard_map/pallas_call | solution.py:463
  78.8 1.5 %add_bitcast_fusion = (f32[3,16,256]{2,1,0:T(8,128)}, f32[3,16,256]{2,1,0:T(8,128)}) fusion(f32[2,2,3,16,256]{4,3,2,1,0:T(8,128)} %shard_map.140), kind=kLoop, calls=%fused_computation | loop fusion | flops 24576 | bytes 294912 | tf_op jit(solution)/shard_map/add | solution.py:517

commit v7 on v6

--- a/solution.py
+++ b/solution.py
@@ -117,6 +117,7 @@
     relay_sem,
     base_send,
     base_recv,
+    base_cross,
     fsend_sem,
     frecv_sem,
     bsend_sem,
@@ -144,26 +145,33 @@
     ]
     for copy in own:
         copy.start()
+    near = 4
+
+    def far_pencil(n):
+        ring = lax.rem(p // near + far_first(n // near, pencils // near), pencils // near)
+        return ring * near + lax.rem(lax.rem(p, near) + lax.rem(n + 1, near), near)
+
+    def far_owner(n):
+        coil = lax.rem(c + far_first(n // frames, coils), coils)
+        return coil, lax.rem(t + lax.rem(n + 1, frames), frames)
+
     barrier = pltpu.get_barrier_semaphore()
 
-    def greet_pencil(d, carry):
-        peer = lax.rem(p + d, pencils)
-        pl.semaphore_signal(barrier, inc=1, device_id={"pencil": peer}, device_id_type=MESH)
+    def greet_owner(n, carry):
+        coil, frame = far_owner(n)
+        pl.semaphore_signal(
+            barrier, inc=1, device_id={"coil": coil, "frame": frame}, device_id_type=MESH
+        )
         return carry
 
-    lax.fori_loop(1, pencils, greet_pencil, 0)
-
-    def greet_maps(d, carry):
-        peer = lax.rem(me + d, coils * frames)
+    def greet_pencil(n, carry):
         pl.semaphore_signal(
-            barrier,
-            inc=1,
-            device_id={"coil": peer // frames, "frame": lax.rem(peer, frames)},
-            device_id_type=MESH,
+            barrier, inc=1, device_id={"pencil": far_pencil(n)}, device_id_type=MESH
         )
         return carry
 
-    lax.fori_loop(1, coils * frames, greet_maps, 0)
+    lax.fori_loop(0, owners - 1, greet_owner, 0)
+    lax.fori_loop(0, pencils - 1, greet_pencil, 0)
 
     pairs = [
         (rows_y_in, rows_y),
@@ -207,16 +215,6 @@
     )
     weight_copy.start()
 
-    near = 4
-
-    def far_pencil(n):
-        ring = lax.rem(p // near + far_first(n // near, pencils // near), pencils // near)
-        return ring * near + lax.rem(lax.rem(p, near) + lax.rem(n + 1, near), near)
-
-    def far_owner(n):
-        coil = lax.rem(c + far_first(n // frames, coils), coils)
-        return coil, lax.rem(t + lax.rem(n + 1, frames), frames)
-
     def images_direct(frame, count):
         def one(n, carry):
             pltpu.make_async_remote_copy(
@@ -262,17 +260,18 @@
                 if (way == 0) == (frame is t):
                     image_copy(block, i, irecv_sem.at[i], c + 2 * step, None)
 
-    def bases_to(d, carry):
-        peer = lax.rem(me + d, owners)
+    def base_copy(owner, sem, device):
+        block = bases.at[owner]
         pltpu.make_async_remote_copy(
-            own_base,
-            bases.at[me],
-            base_send,
-            base_recv,
-            device_id={"coil": peer // frames, "frame": lax.rem(peer, frames)},
-            device_id_type=MESH,
+            block, block, base_send, sem, device_id=device, device_id_type=MESH
         ).start()
-        return carry
+
+    def bases_along(owner):
+        def one(n, carry):
+            base_copy(owner, base_recv, {"coil": lax.rem(c + far_first(n, coils), coils)})
+            return carry
+
+        lax.fori_loop(0, coils - 1, one, 0)
 
     slabs = [(h, i) for h in range(halves) for i in range(1, planes)]
     parts = [(slice(None), 0), *slabs]
@@ -354,11 +353,16 @@
         if i == 0:
             for later in range(1, planes):
                 relay(later)
-    lax.fori_loop(1, owners, bases_to, 0)
+    base_copy(me, base_cross, {"frame": other})
+    bases_along(me)
 
     for copy in loads[3:6]:
         copy.wait()
     all_but_one(recv_f, parts[0], frecv_sem.at[0])
+    partner = c * frames + other
+    crossed = bases.at[partner]
+    pltpu.make_async_copy(crossed, crossed, base_cross).wait()
+    bases_along(partner)
     lines = jnp.concatenate(
         [recv_f[:, h, 0].reshape(-1, width) for h in range(halves)], axis=1
     )
@@ -389,7 +393,8 @@
 
     loads[7].wait()
     base_blocks = bases.at[pl.ds(0, owners - 1)]
-    pltpu.make_async_copy(base_blocks, base_blocks, base_recv).wait()
+    along_blocks = bases.at[pl.ds(0, owners - frames)]
+    pltpu.make_async_copy(along_blocks, along_blocks, base_recv).wait()
     for i in range(planes):
         for h in range(halves):
             all_but_one(recv_b, (h, i), brecv_sem.at[h * planes + i])
@@ -491,6 +496,7 @@
                 dma((planes, frames, 2)),
                 dma,
                 dma,
+                dma,
                 dma((1 + halves * (planes - 1),)),
                 dma((1 + halves * (planes - 1),)),
                 dma((planes * halves,)),

time: 80.5 us -> 79.6 us (0.989)
  Pallas kernels: 76.9 us -> 76 us
    pallas_call x1, Pallas kernels: 76.9 us -> 76 us  [per_device(): pl.pallas_call(lambda *refs: kernel((coils, pencils, frames), *refs), out...]
where the time goes in v7:
time: 79.6 us; the launch traced here: 79.5 us
  Pallas kernels  76 us (95%)
  between operations  1.93 us (2%)
  other arithmetic  1.52 us (2%)
    pallas_call x1, Pallas kernels, per_device(): pl.pallas_call(lambda *refs: kernel((coils, pencils, frames), *refs), out...  76 us

profile of v7, /device:TPU:1, one launch (start us, length us, event | category | flops | bytes accessed | tf_op | source)
XLA Modules:
  0.0 79.5 jit_solution(2394875832083775540)
XLA Ops:
  1.9 76.0 %shard_map.140 = f32[2,2,3,16,256]{4,3,2,1,0:T(8,128)} custom-call(bf16[2,3,16,256]{3,2,1,0:T(8,128)(2,1)} %refs_0_.1, bf16[3,16,256]{2,1,0:T(8,128)(2,1)} %refs_1_.1, bf16[3,16,256]{2,1,0:T(8,128)(2,1)} %refs_2_.1, f32[1]{0:T(128)S(6)} %copy.15.refs_3_, f32[1]{0:T(128)S(6)} %copy.16.refs_4_, bf16[2,3,256,256]{3,2,1,0:T(8,128)(2,1)} %bitcast.7, ...), custom_call_target="tpu_custom_call" | custom-call | tf_op jit(solution)/shard_map/pallas_call | solution.py:468
  77.9 1.5 %add_bitcast_fusion = (f32[3,16,256]{2,1,0:T(8,128)}, f32[3,16,256]{2,1,0:T(8,128)}) fusion(f32[2,2,3,16,256]{4,3,2,1,0:T(8,128)} %shard_map.140), kind=kLoop, calls=%fused_computation | loop fusion | flops 24576 | bytes 294912 | tf_op jit(solution)/shard_map/add | solution.py:523

commit v8 on v7

--- a/solution.py
+++ b/solution.py
@@ -354,11 +354,11 @@
             for later in range(1, planes):
                 relay(later)
     base_copy(me, base_cross, {"frame": other})
-    bases_along(me)
 
     for copy in loads[3:6]:
         copy.wait()
     all_but_one(recv_f, parts[0], frecv_sem.at[0])
+    bases_along(me)
     partner = c * frames + other
     crossed = bases.at[partner]
     pltpu.make_async_copy(crossed, crossed, base_cross).wait()

time: 79.6 us -> 79.9 us (level)
  no operation moved by 1% of the time
where the time goes in v8:
time: 79.9 us; the launch traced here: 79.7 us
  Pallas kernels  76.3 us (95%)
  between operations  1.93 us (2%)
  other arithmetic  1.52 us (2%)
    pallas_call x1, Pallas kernels, per_device(): pl.pallas_call(lambda *refs: kernel((coils, pencils, frames), *refs), out...  76.3 us

profile of v8, /device:TPU:1, one launch (start us, length us, event | category | flops | bytes accessed | tf_op | source)
XLA Modules:
  0.0 79.7 jit_solution(13149608978182044487)
XLA Ops:
  1.9 76.3 %shard_map.140 = f32[2,2,3,16,256]{4,3,2,1,0:T(8,128)} custom-call(bf16[2,3,16,256]{3,2,1,0:T(8,128)(2,1)} %refs_0_.1, bf16[3,16,256]{2,1,0:T(8,128)(2,1)} %refs_1_.1, bf16[3,16,256]{2,1,0:T(8,128)(2,1)} %refs_2_.1, f32[1]{0:T(128)S(6)} %copy.15.refs_3_, f32[1]{0:T(128)S(6)} %copy.16.refs_4_, bf16[2,3,256,256]{3,2,1,0:T(8,128)(2,1)} %bitcast.7, ...), custom_call_target="tpu_custom_call" | custom-call | tf_op jit(solution)/shard_map/pallas_call | solution.py:468
  78.2 1.5 %add_bitcast_fusion = (f32[3,16,256]{2,1,0:T(8,128)}, f32[3,16,256]{2,1,0:T(8,128)}) fusion(f32[2,2,3,16,256]{4,3,2,1,0:T(8,128)} %shard_map.140), kind=kLoop, calls=%fused_computation | loop fusion | flops 24576 | bytes 294912 | tf_op jit(solution)/shard_map/add | solution.py:523
